TPU v7x, 512 devices: a whole 4x4x16 slice. The times are simulated.
512 devices in a mesh: pts: 256 (over x, y, z), rep: 2 (over core).
Axes of the slice: x: 4, y: 4, z: 16, core: 2. Of those that a mesh axis runs over, the one named last changes fastest.
Arguments:
- points: bfloat16 [262144, 256], P(('pts', 'rep')), may hold values from -6 to 6
- out_grad: bfloat16 [262144, 256], P(('pts', 'rep')), may hold values from -8 to 8
- ln_gain: float32 [256], replicated, may hold values from 0.5 to 1.5
- ln_bias: float32 [256], replicated, may hold values from -3 to 3
- w_mid: bfloat16 [256, 256], replicated, may hold values from -0.375 to 0.375
- w_feat: bfloat16 [256, 256], replicated, may hold values from -0.375 to 0.375
- w_slice: bfloat16 [32, 64], replicated, may hold values from -1 to 1
- temper: float32 [8], replicated, may hold values from 0.3 to 1.5
- query_weight: float32 [32, 32], replicated, may hold values from -1 to 1
- key_weight: float32 [32, 32], replicated, may hold values from -1 to 1
- value_weight: float32 [32, 32], replicated, may hold values from -1 to 1
- w_out: bfloat16 [256, 256], replicated, may hold values from -0.375 to 0.375
Outputs:
- grad_points: bfloat16 [262144, 256], P(('pts', 'rep'))
- grad_gain: float32 [256], replicated
- grad_bias: float32 [256], replicated
- grad_mid: float32 [256, 256], P('rep')
- grad_feat: float32 [256, 256], P('rep')
- grad_slice: float32 [32, 64], replicated
- grad_temper: float32 [8], replicated
- grad_query: float32 [32, 32], replicated
- grad_key: float32 [32, 32], replicated
- grad_value: float32 [32, 32], replicated
- output_weight_gradient: float32 [256, 256], P('rep')
All inputs are finite; a program needn't handle non-finite values.
Results may differ from a plain program's by a relative error of at most 0.013.
The roundings to bfloat16 on the way count: a program that leaves them out, or rounds other values in their place, can miss the bound.
Values sent between devices are 32-bit elements; how exact they have to be, the bound alone decides.
A program may use at most 64 MiB of HBM per device.

v0:
```python
import jax
import jax.numpy as jnp
from jax import lax
from jax.sharding import PartitionSpec as P


def layer_norm(values, ln_gain, ln_bias):
    center = values - jnp.mean(values, axis=-1, keepdims=True)
    spread = jnp.mean(center * center, axis=-1, keepdims=True)
    return center * lax.rsqrt(spread + 1e-05) * ln_gain + ln_bias


def token_mix(slice_tokens, query_weight, key_weight, value_weight):
    highest_precision = lax.Precision.HIGHEST
    query_rows = jnp.einsum("ytj,jv->ytv", slice_tokens, query_weight, precision=highest_precision)
    slice_key_rows = jnp.einsum(
        "ytj,jv->ytv", slice_tokens, key_weight, precision=highest_precision
    )
    slice_value_rows = jnp.einsum(
        "ytj,jv->ytv", slice_tokens, value_weight, precision=highest_precision
    )
    scores = jnp.einsum(
        "hme,hne->hmn", query_rows, slice_key_rows, precision=highest_precision
    ) * slice_tokens.shape[-1] ** (-0.5)
    powers = jnp.exp(scores)
    attention = powers / jnp.sum(powers, axis=-1, keepdims=True)
    return jnp.einsum("hmn,hne->hme", attention, slice_value_rows, precision=highest_precision)


def shards(
    points,
    out_grad,
    ln_gain,
    ln_bias,
    w_mid,
    w_feat,
    w_slice,
    temper,
    query_weight,
    key_weight,
    value_weight,
    w_out,
):
    highest_precision = lax.Precision.HIGHEST
    row_count = points.shape[0]
    feat_width = points.shape[1]
    head_count = temper.shape[0]
    head_dim = feat_width // head_count
    slices = w_slice.shape[1]
    everyone = row_count * lax.axis_size("pts") * lax.axis_size("rep")
    normed_full, ln_back = jax.vjp(layer_norm, points.astype(jnp.float32), ln_gain, ln_bias)
    normed = normed_full.astype(jnp.bfloat16)
    middle = jnp.dot(normed, w_mid, preferred_element_type=jnp.float32).astype(jnp.bfloat16)
    feature = jnp.dot(normed, w_feat, preferred_element_type=jnp.float32).astype(jnp.bfloat16)
    mid_heads = middle.reshape(row_count, head_count, head_dim)
    feature_per_head = feature.reshape(row_count, head_count, head_dim)
    logits = (
        jnp.einsum("nhd,dm->nhm", mid_heads, w_slice, preferred_element_type=jnp.float32)
        / temper[None, :, None]
    )
    powers = jnp.exp(logits)
    weights = powers / jnp.sum(powers, axis=-1, keepdims=True)
    slice_weight = weights.astype(jnp.bfloat16)
    totals_part = jnp.einsum(
        "wfr,wfy->fry", slice_weight, feature_per_head, preferred_element_type=jnp.float32
    )
    masses_part = jnp.sum(slice_weight, axis=0, dtype=jnp.float32)
    output_per_head = w_out.astype(jnp.float32).reshape(head_count, head_dim, feat_width)
    flat_w = slice_weight.reshape(row_count, head_count * slices)
    slice_totals, masses = lax.psum((totals_part, masses_part), ("pts", "rep"))
    slice_tokens = slice_totals / (masses[..., None] + 1e-05)
    mixed_full, mix_back = jax.vjp(token_mix, slice_tokens, query_weight, key_weight, value_weight)
    slice_tokens, mixed_bfloat, mix_back = (slice_tokens, mixed_full.astype(jnp.bfloat16), mix_back)
    summed = jnp.einsum("nk,nc->kc", flat_w, out_grad, preferred_element_type=jnp.float32)
    projected_share = summed.reshape(head_count, slices, feat_width)
    mixed_gradient = lax.psum(
        jnp.einsum("nov,njv->noj", projected_share, output_per_head, precision=highest_precision),
        ("pts", "rep"),
    )
    out_term = jnp.einsum(
        "zgo,zgl->zol",
        mixed_bfloat.astype(jnp.float32),
        projected_share,
        precision=highest_precision,
    ).reshape(feat_width, feat_width)
    d_tokens, grad_query, grad_key, grad_value = mix_back(mixed_gradient)
    masses_gradient = -jnp.sum(d_tokens * slice_tokens, axis=-1) / (masses + 1e-05)
    totals_gradient = (d_tokens / (masses[..., None] + 1e-05)).astype(jnp.bfloat16)
    d_desliced = jnp.einsum(
        "nc,kc->nk", out_grad, w_out, preferred_element_type=jnp.float32
    ).astype(jnp.bfloat16)
    desliced_per_head = d_desliced.reshape(row_count, head_count, head_dim)
    weights_gradient = (
        jnp.einsum(
            "xbs,bqs->xbq", desliced_per_head, mixed_bfloat, preferred_element_type=jnp.float32
        )
        + jnp.einsum(
            "xbs,bqs->xbq", feature_per_head, totals_gradient, preferred_element_type=jnp.float32
        )
        + masses_gradient[None]
    )
    feature_gradient = (
        jnp.einsum(
            "ztl,tlw->ztw", slice_weight, totals_gradient, preferred_element_type=jnp.float32
        )
        .astype(jnp.bfloat16)
        .reshape(row_count, feat_width)
    )
    d_logits = weights * (
        weights_gradient - jnp.sum(weights_gradient * weights, axis=-1, keepdims=True)
    )
    scaled = (d_logits / temper[None, :, None]).astype(jnp.bfloat16)
    d_mid = (
        jnp.einsum("nhm,dm->nhd", scaled, w_slice, preferred_element_type=jnp.float32)
        .astype(jnp.bfloat16)
        .reshape(row_count, feat_width)
    )
    slice_part = jnp.einsum("nhd,nhm->dm", mid_heads, scaled, preferred_element_type=jnp.float32)
    temper_part = -jnp.sum(d_logits * logits, axis=(0, 2)) / temper
    mid_part = jnp.einsum("nc,nk->ck", normed, d_mid, preferred_element_type=jnp.float32)
    feat_part = jnp.einsum(
        "nc,nk->ck", normed, feature_gradient, preferred_element_type=jnp.float32
    )
    d_normed = jnp.einsum(
        "nk,ck->nc", d_mid, w_mid, preferred_element_type=jnp.float32
    ) + jnp.einsum("nk,ck->nc", feature_gradient, w_feat, preferred_element_type=jnp.float32)
    d_values, gain_part, bias_part = ln_back(d_normed)
    stacked = jnp.stack([mid_part, feat_part, out_term])
    halves = lax.psum_scatter(stacked, "rep", scatter_dimension=1, tiled=True)
    halves = lax.psum(halves, "pts")
    small_sums = lax.psum((slice_part, temper_part, gain_part, bias_part), ("pts", "rep"))
    out_rows = halves[2] / everyone
    return (
        d_values.astype(jnp.bfloat16),
        small_sums[2] / everyone,
        small_sums[3] / everyone,
        halves[0] / everyone,
        halves[1] / everyone,
        small_sums[0] / everyone,
        small_sums[1] / everyone,
        grad_query / everyone,
        grad_key / everyone,
        grad_value / everyone,
        out_rows,
    )


def solution(mesh):
    in_specs = (
        P(("pts", "rep"), None),
        P(("pts", "rep"), None),
        P(),
        P(),
        P(),
        P(),
        P(),
        P(),
        P(),
        P(),
        P(),
        P(),
    )
    out_specs = (
        P(("pts", "rep"), None),
        P(),
        P(),
        P("rep", None),
        P("rep", None),
        P(),
        P(),
        P(),
        P(),
        P(),
        P("rep", None),
    )
    return jax.shard_map(shards, mesh=mesh, in_specs=in_specs, out_specs=out_specs, check_vma=False)
```

profile of v0, /device:TPU:1, one launch (start us, length us, event | category | flops | bytes accessed | tf_op | source)
XLA Modules:
  0.0 982.1 jit_solution(10095997772667257541)
XLA Ops:
  7.2 1.2 convert_reduce_fusion.1
  8.7 0.6 copy-done.5
  9.4 0.4 convolution_convert_fusion.3
  9.8 0.5 copy-done.3
  10.3 0.4 convolution_convert_fusion.4
  11.0 0.4 copy-done.27
  11.4 0.4 exponential_reduce_fusion
  12.1 0.3 copy-done.16
  12.4 0.9 fusion.51
  13.6 0.6 copy-done.2
  14.2 1.1 fusion.53
  15.6 111.5 %psum.57 = f32[8,64]{1,0:T(8,128)S(1)} all-reduce(f32[8,64]{1,0:T(8,128)S(1)} %get-tuple-element.22), channel_id=1, replica_groups=mesh['pts'=256,'rep'=2] {'pts','rep'}, use_global_device_ids=true, to_apply=%region_5.0 | all-reduce | flops 512 | bytes 4096 | tf_op jit(solution)/shard_map/psum | solution.py:70
  127.1 349.9 %all-reduce.7.cloned.1.call-done = (f32[8,64,32]{1,2,0:T(8,128)}, f32[8,64,32]{1,2,0:T(8,128)}) async-done(((f32[8,64,32]{1,2,0:T(8,128)}, f32[8,64,32]{1,2,0:T(8,128)}), (f32[8,64,32]{1,2,0:T(8,128)}, f32[8,64,32]{1,2,0:T(8,128)})) %all-reduce.7.cloned.1.call-update) | async-done | bytes 131088 | tf_op jit(solution)/shard_map/psum | solution.py:70
  477.1 1.3 fusion.33
  478.4 0.3 fusion.30
  478.7 0.4 copy-done.20
  479.1 0.3 fusion.36
  479.4 0.6 fusion.50
  480.1 0.4 convolution_convert_fusion.5
  480.4 0.5 copy-done.9
  481.0 0.5 fusion.27
  481.5 0.6 multiply_reduce_fusion.2
  482.2 0.4 fusion.41
  482.6 0.6 fusion.42
  483.2 0.3 fusion.55
  484.6 0.3 fusion.52
  485.0 0.4 fusion.4
  485.3 0.3 copy-done.17
  485.7 0.5 multiply_reduce_fusion
  486.4 0.4 copy-done.22
  487.1 0.5 copy-done.26
  487.8 0.4 convolution_bitcast_fusion.1
  488.2 0.5 copy-done.4
  488.9 0.4 convolution_bitcast_fusion
  489.4 0.9 pad_maximum_fusion
  490.4 0.8 copy-done.6
  491.2 0.5 fusion.18
  491.7 103.1 %all-reduce = (f32[256]{0:T(256)S(1)}, f32[256]{0:T(256)S(1)}, f32[32,64]{1,0:T(8,128)S(1)}, f32[8]{0:T(128)S(1)}) all-reduce(f32[256]{0:T(256)S(1)} %get-tuple-element.11, f32[256]{0:T(256)S(1)} %get-tuple-element.13, f32[32,64]{1,0:T(8,128)S(1)} %convolution_bitcast_fusion.5, ...), channel_id=1, replica_groups=mesh['pts'=256,'rep'=2] {'pts','rep'}, use_global_device_ids=true, to_apply=%region_14.0 | all-reduce | flops 2568 | bytes 20544 | tf_op jit(solution)/shard_map/psum | solution.py:131
  594.8 0.4 fusion.48
  595.2 0.6 broadcast_multiply_fusion.2
  595.7 0.6 broadcast_multiply_fusion
  596.4 0.9 fusion.7
  597.3 0.9 fusion.8
  598.2 0.9 fusion.6
  599.0 0.5 broadcast_multiply_fusion.4
  599.6 0.8 add_convert_fusion
  600.4 373.4 %all-reduce.5.cloned.1.call-done = f32[3,128,256]{2,1,0:T(8,128)} async-done(((f32[3,128,256]{2,1,0:T(8,128)}), f32[3,128,256]{2,1,0:T(8,128)}) %all-reduce.5.cloned.1.call-update) | async-done | bytes 393232 | tf_op jit(solution)/shard_map/psum | solution.py:130
  973.8 1.8 fusion.24
  (73 shorter events, 3.7 us)
Async XLA Ops:
  7.2 6.2 copy-start
  7.2 1.2 copy-start.1
  7.2 469.8 %all-reduce.7.cloned.1.call-start = ((), (), s32[]{:S(2)}) async-start(), calls=%async_computation.3 | async-start | bytes 524288 | tf_op jit(solution)/shard_map/psum | solution.py:70
  8.4 0.9 copy-start.5
  8.7 0.7 copy-start.23
  8.7 0.7 copy-start.25
  9.4 0.9 copy-start.3
  10.3 0.7 copy-start.21
  10.7 0.7 copy-start.27
  11.8 0.6 copy-start.16
  13.3 0.9 copy-start.2
  15.3 583.7 %reduce-scatter.2.cloned.1.call-start = ((), (), s32[]{:S(2)}) async-start(), calls=%async_computation.1 | async-start | bytes 1179648 | tf_op jit(solution)/shard_map/reduce_scatter | solution.py:129
  15.6 461.4 %copy-start.19 = (f32[32,32]{1,0:T(8,128)S(1)}, f32[32,32]{1,0:T(8,128)}, u32[]{:S(2)}) copy-start(f32[32,32]{1,0:T(8,128)} %param.21) | copy-start | bytes 12292
  477.0 1.3 copy-start.12
  477.1 1.3 copy-start.18
  478.4 0.7 copy-start.20
  480.1 0.9 copy-start.9
  481.5 2.0 copy-start.10
  482.6 1.5 copy-start.14
  483.2 0.7 copy-start.7
  484.9 0.7 copy-start.17
  484.9 0.7 copy-start.28
  486.2 0.7 copy-start.22
  486.9 0.7 copy-start.26
  487.1 0.7 copy-start.24
  487.8 0.9 copy-start.4
  490.3 0.9 copy-start.6
  490.3 483.5 %all-reduce.5.cloned.1.call-start = ((), (), s32[]{:S(2)}) async-start(), calls=%async_computation.2 | async-start | bytes 786432 | tf_op jit(solution)/shard_map/psum | solution.py:130
  594.8 1.6 copy-start.8
  594.8 1.6 copy-start.13
  596.3 0.9 copy-start.15
  597.3 0.9 copy-start.11
Sparse Core Ops, SparseCore 0:
  15.4 461.5 all-reduce.6
  490.5 17.0 reduce-scatter.1
  599.2 374.5 all-reduce.4
where the time goes:
time: 992 us; the launch traced here: 982 us
  waiting for transfers between devices  723 us (73%)
  blocking collectives  215 us (22%)
  matrix products  15.4 us (2%)
  between operations  14.2 us (1%)
    psum x1, waiting for transfers between devices, shards(): halves = lax.psum(halves, 'pts')  373 us
    psum x1, waiting for transfers between devices, shards(): slice_totals, masses = lax.psum((totals_part, masses_part), ('pts', 'rep'))  350 us
    psum x1, blocking collectives, shards(): slice_totals, masses = lax.psum((totals_part, masses_part), ('pts', 'rep'))  111 us
    psum x1, blocking collectives, shards(): lax.psum((slice_part, temper_part, gain_part, bias_part), ('pts', 'rep'))  103 us
  transfers between devices with their start and end apart: 3, of which 2 were waited for; matrix products, arithmetic and copies ran while one was open for 1% of the time, Pallas kernels for 0%

commit v1 on v0

v1 whole, which is shorter than its diff:
```python
import functools

import jax
import jax.numpy as jnp
from jax import lax
from jax.experimental import pallas as pl
from jax.experimental.pallas import tpu as pltpu
from jax.sharding import PartitionSpec as P

MESH = pl.DeviceIdType.MESH
F32, BF16 = jnp.float32, jnp.bfloat16
HI = lax.Precision.HIGHEST

HEADS, SLICES, DIM = 8, 64, 32
WIDTH = HEADS * DIM
COLS = HEADS * SLICES
NX, NY, NZ, NC = 4, 4, 16, 2
NXY = NX * NY
LOW = 4
NZH = NZ // LOW
PLANE = NXY * LOW
ROWS1, ROWS2 = 9, 13
SMALL = 40
BF_MAX = 3.3895314e38


def dot(a, b, ca=1, cb=0, precision=None):
    return lax.dot_general(
        a, b, (((ca,), (cb,)), ((), ())), preferred_element_type=F32, precision=precision
    )


def iota(shape, dim):
    return lax.broadcasted_iota(jnp.int32, shape, dim)


def split(values):
    high = values.astype(BF16)
    return high, (values - high.astype(F32)).astype(BF16)


def group_sum(high, low, ones):
    parts = []
    for g in range(0, COLS, 256):
        parts.append(dot(high[:, g : g + 256], ones) + dot(low[:, g : g + 256], ones))
    return jnp.concatenate(parts, axis=1)


def block_diagonal(tile_t):
    whole = jnp.concatenate([tile_t] * HEADS, axis=0)
    own = iota((WIDTH, COLS), 0) // DIM == iota((WIDTH, COLS), 1) // SLICES
    return jnp.where(own, whole, 0.0)


def diagonal_rows(full):
    left = iota((DIM, 128), 1) < SLICES
    parts = []
    for g in range(HEADS // 2):
        cols = slice(128 * g, 128 * g + 128)
        parts.append(
            jnp.where(
                left,
                full[2 * DIM * g : 2 * DIM * g + DIM, cols],
                full[2 * DIM * g + DIM : 2 * DIM * g + 2 * DIM, cols],
            )
        )
    return parts


def token_step(totals, masses, d_mixed, wq, wk, wv):
    scale = DIM ** (-0.5)
    inv = 1.0 / (masses + 1e-05)
    tokens = totals * inv
    q = dot(wq, tokens, 0, 0, HI)
    k = dot(wk, tokens, 0, 0, HI)
    v = dot(wv, tokens, 0, 0, HI)
    same = iota((128, 128), 0) // SLICES == iota((128, 128), 1) // SLICES
    mixed, dq, dk, dv = [], [], [], []
    for g in range(HEADS // 2):
        cols = slice(128 * g, 128 * g + 128)
        qg, kg, vg, dmg = q[:, cols], k[:, cols], v[:, cols], d_mixed[:, cols]
        powers = jnp.where(same, jnp.exp(dot(qg, kg, 0, 0, HI) * scale), 0.0)
        att = powers / jnp.sum(powers, axis=1, keepdims=True)
        mixed.append(dot(vg, att, 1, 1, HI))
        dv.append(dot(dmg, att, 1, 0, HI))
        d_att = dot(dmg, vg, 0, 0, HI)
        d_scores = att * (d_att - jnp.sum(d_att * att, axis=1, keepdims=True)) * scale
        dq.append(dot(kg, d_scores, 1, 1, HI))
        dk.append(dot(qg, d_scores, 1, 0, HI))
    join = functools.partial(jnp.concatenate, axis=1)
    mixed, dq, dk, dv = join(mixed), join(dq), join(dk), join(dv)
    d_tokens = dot(wq, dq, 1, 0, HI) + dot(wk, dk, 1, 0, HI) + dot(wv, dv, 1, 0, HI)
    grads = [dot(tokens, d, 1, 1, HI) for d in (dq, dk, dv)]
    d_masses = -jnp.sum(d_tokens * tokens, axis=0, keepdims=True) * inv
    return mixed, d_tokens * inv, d_masses, grads


def kernel(
    everyone,
    chunk,
    points,
    out_grad,
    gain_ref,
    bias_ref,
    w_mid,
    w_feat,
    w_slice,
    temper,
    wq,
    wk,
    wv,
    w_out,
    o_points,
    o_gain,
    o_bias,
    o_mid,
    o_feat,
    o_slice,
    o_temper,
    o_q,
    o_k,
    o_v,
    o_out,
    xhat_s,
    rstd_s,
    normed_s,
    mid_s,
    fd_s,
    low_s,
    logits_s,
    w_s,
    sw_s,
    sc_s,
    dmf_s,
    ds_s,
    p1,
    r10,
    a1,
    r11,
    r12,
    r13,
    p2,
    r20,
    a2,
    r21,
    r22,
    c2,
    r23,
    sends,
    recvs,
):
    p, c = lax.axis_index("pts"), lax.axis_index("rep")
    xy, z = p // NZ, p % NZ
    zl, zh = z % LOW, z // LOW
    rows = points.shape[0]

    def at(xy_, z_, c_):
        return (xy_ * NZ + z_, c_)

    def plane_core(j):
        t = (xy * NC + c + j) % (NXY * NC)
        return at(t // NC, z, t % NC)

    def plane(j):
        return at((xy + j) % NXY, z, c)

    def column(j):
        return at(xy, (z + j) % NZ, c)

    def block(j):
        t = (xy * LOW + zl + j) % PLANE
        return at(t // LOW, zh * LOW + t % LOW, c)

    def block_other(j):
        return at((xy + 1 + j // (LOW - 1)) % NXY, zh * LOW + (zl + 1 + j % (LOW - 1)) % LOW, c)

    def column_high(j):
        return at(xy, (z + LOW * j) % NZ, c)

    sibling = (p, 1 - c)

    barrier = pltpu.get_barrier_semaphore()

    def greet(who, first, last):
        def body(j, _):
            pl.semaphore_signal(barrier, inc=1, device_id=who(j), device_id_type=MESH)
            return 0

        lax.fori_loop(first, last, body, 0)

    n_other = (NXY - 1) * (LOW - 1)
    greet(plane_core, 1, NXY * NC)
    greet(column, 1, NZ)
    greet(block_other, 0, n_other)

    def send_all(stage, who, count, src, dst):
        def body(j, _):
            pltpu.make_async_remote_copy(
                src(j), dst, sends.at[stage], recvs.at[stage], device_id=who(j), device_id_type=MESH
            ).start()
            return 0

        lax.fori_loop(1, count + 1, body, 0)

    def wait_recv(stage, ref):
        pltpu.make_async_remote_copy(
            ref, ref, sends.at[stage], recvs.at[stage], device_id=sibling, device_id_type=MESH
        ).wait_recv()

    def wait_send(stage, ref):
        pltpu.make_async_remote_copy(
            ref, ref, sends.at[stage], recvs.at[stage], device_id=sibling, device_id_type=MESH
        ).wait_send()

    gain, bias = gain_ref[...], bias_ref[...]
    head_of = iota((1, COLS), 1) // SLICES
    temper_row = jnp.zeros((1, COLS), F32)
    for h in range(HEADS):
        temper_row = jnp.where(head_of == h, temper[h], temper_row)
    inv_t = 1.0 / temper_row
    ones = (iota((256, 256), 0) // SLICES == iota((256, 256), 1) // SLICES).astype(F32).astype(BF16)
    ws = w_slice[...].astype(F32)
    slice_blocks = block_diagonal(jnp.concatenate([ws] * HEADS, axis=1)).astype(BF16)

    for r in range(0, rows, chunk):
        here = pl.ds(r, chunk)
        x = points[here, :].astype(F32)
        center = x - jnp.mean(x, axis=1, keepdims=True)
        rstd = lax.rsqrt(jnp.mean(center * center, axis=1, keepdims=True) + 1e-05)
        xhat = center * rstd
        xhat_s[here, :] = xhat
        rstd_s[here, :] = jnp.broadcast_to(rstd, (chunk, 128))
        normed = (xhat * gain + bias).astype(BF16)
        normed_s[here, :] = normed
        mid = dot(normed, w_mid[...]).astype(BF16)
        mid_s[here, :] = mid
        fd_s[here, WIDTH:] = dot(normed, w_feat[...]).astype(BF16)
        logits = dot(mid, slice_blocks) * inv_t
        logits_s[here, :] = logits
        powers = jnp.exp(logits)
        high = jnp.minimum(powers, BF_MAX).astype(BF16)
        low = (powers - high.astype(F32)).astype(BF16)
        weights = powers / group_sum(high, low, ones)
        w_s[here, :] = weights
        sw_s[here, :] = weights.astype(BF16)
        d_high, d_low = split(dot(out_grad[here, :], w_out[...], 1, 1))
        fd_s[here, :WIDTH] = d_high
        low_s[here, :] = d_low

    sw = sw_s[...]
    by_fd = dot(fd_s[...], sw, 0, 0)
    by_low = dot(low_s[...], sw, 0, 0)
    tot = diagonal_rows(by_fd[WIDTH:])
    dmx = diagonal_rows(by_fd[:WIDTH] + by_low)
    mass = dot(jnp.ones((8, rows), BF16), sw)[:1]
    quarter = iota((1, 128), 1) // DIM
    for i in range(4):
        for j in range(4):
            k = 4 * i + j
            p1[0, k, 0:8, :] = tot[j][8 * i : 8 * i + 8]
            p1[1, k, 0:8, :] = dmx[j][8 * i : 8 * i + 8]
            p1[0, k, 8:9, :] = jnp.where(quarter == i, mass[:, 128 * j : 128 * j + 128], 0.0)
            p1[1, k, 8:9, :] = jnp.zeros((1, 128), F32)

    pl.semaphore_wait(barrier, NXY * NC - 1 + NZ - 1 + n_other)

    pltpu.make_async_remote_copy(
        p1.at[1 - c], r10, sends.at[0], recvs.at[0], device_id=sibling, device_id_type=MESH
    ).start()
    wait_recv(0, r10)
    a1[...] = p1[c] + r10[...]
    send_all(1, plane, NXY - 1, lambda j: a1.at[(xy + j) % NXY], r11.at[xy])
    r11[xy] = a1[xy]
    wait_recv(1, r11.at[pl.ds(0, NXY - 1)])
    r12[z] = jnp.sum(r11[...], axis=0)
    send_all(2, column, NZ - 1, lambda j: r12.at[z], r12.at[z])
    wait_recv(2, r12.at[pl.ds(0, NZ - 1)])
    me1 = c * NXY + xy
    r13[me1] = jnp.sum(r12[...], axis=0)
    send_all(3, plane_core, NXY * NC - 1, lambda j: r13.at[me1], r13.at[me1])
    wait_recv(3, r13.at[pl.ds(0, NXY * NC - 1)])

    def whole(half):
        return jnp.concatenate(
            [
                jnp.concatenate([r13[NXY * half + 4 * i + j, 0:8, :] for i in range(4)], axis=0)
                for j in range(4)
            ],
            axis=1,
        )

    masses = jnp.concatenate(
        [sum(r13[4 * i + j, 8:9, :] for i in range(4)) for j in range(4)], axis=1
    )
    mixed, d_totals, d_masses, grads = token_step(
        whole(0), masses, whole(1), wq[...], wk[...], wv[...]
    )
    for out, grad in zip((o_q, o_k, o_v), grads):
        out[...] = grad / everyone
    both = jnp.concatenate(
        [
            block_diagonal(mixed.astype(BF16).astype(F32)).astype(BF16),
            block_diagonal(d_totals.astype(BF16).astype(F32)).astype(BF16),
        ],
        axis=0,
    )
    w_both = jnp.concatenate([w_mid[...], w_feat[...]], axis=1)

    temper_sum = jnp.zeros((8, COLS), F32)
    gain_sum = jnp.zeros((8, WIDTH), F32)
    bias_sum = jnp.zeros((8, WIDTH), F32)

    def fold(values):
        return jnp.sum(values.reshape(values.shape[0] // 8, 8, values.shape[1]), axis=0)

    for r in range(0, rows, chunk):
        here = pl.ds(r, chunk)
        weights = w_s[here, :]
        d_weights = dot(fd_s[here, :], both) + d_masses
        high, low = split(d_weights * weights)
        d_logits = weights * (d_weights - group_sum(high, low, ones))
        scaled = (d_logits * inv_t).astype(BF16)
        sc_s[here, :] = scaled
        temper_sum += fold(d_logits * logits_s[here, :])
        d_mid = dot(scaled, slice_blocks, 1, 1).astype(BF16)
        by_both = dot(sw_s[here, :], both, 1, 1)
        d_feat = by_both[:, WIDTH:].astype(BF16)
        s_high, s_low = split(by_both[:, :WIDTH])
        ds_s[here, :WIDTH] = s_high
        ds_s[here, WIDTH:] = s_low
        dmf_s[here, :WIDTH] = d_mid
        dmf_s[here, WIDTH:] = d_feat
        d_normed = dot(dmf_s[here, :], w_both, 1, 1)
        xhat = xhat_s[here, :]
        gain_sum += fold(d_normed * xhat)
        bias_sum += fold(d_normed)
        d_xhat = d_normed * gain
        inner = d_xhat - jnp.mean(d_xhat, axis=1, keepdims=True)
        inner = inner - xhat * jnp.mean(d_xhat * xhat, axis=1, keepdims=True)
        o_points[here, :] = (inner * rstd_s[here, 0:1]).astype(BF16)

    by_normed = dot(normed_s[...], dmf_s[...], 0, 0)
    by_slices = dot(ds_s[...], out_grad[...], 0, 0)
    out_w = by_slices[:WIDTH] + by_slices[WIDTH:]
    slice_sum = sum(diagonal_rows(dot(mid_s[...], sc_s[...], 0, 0)))
    small = jnp.concatenate(
        [jnp.sum(gain_sum, axis=0, keepdims=True)[:, 128 * l : 128 * l + 128] for l in range(2)]
        + [jnp.sum(bias_sum, axis=0, keepdims=True)[:, 128 * l : 128 * l + 128] for l in range(2)]
        + [jnp.sum(temper_sum, axis=0, keepdims=True)[:, 128 * l : 128 * l + 128] for l in range(4)]
        + [slice_sum],
        axis=0,
    )
    for h in range(NC):
        half = slice(128 * h, 128 * h + 128)
        for a in range(2):
            for l in range(2):
                first = WIDTH * a + 128 * l
                p2[h, 32 * a + 16 * l : 32 * a + 16 * l + 16, 0:8, :] = by_normed[
                    half, first : first + 128
                ].reshape(16, 8, 128)
        for l in range(2):
            for s in range(32):
                p2[h, 32 * l + s, 8:12, :] = out_w[
                    128 * h + 4 * s : 128 * h + 4 * s + 4, 128 * l : 128 * l + 128
                ]
        for k in range(PLANE):
            p2[h, k, 12:13, :] = small[k : k + 1] if k < SMALL else jnp.zeros((1, 128), F32)

    pltpu.make_async_remote_copy(
        p2.at[1 - c], r20, sends.at[4], recvs.at[4], device_id=sibling, device_id_type=MESH
    ).start()
    wait_recv(4, r20)
    a2[...] = p2[c] + r20[...]
    t = xy * LOW + zl
    send_all(5, block, PLANE - 1, lambda j: a2.at[(t + j) % PLANE], r21.at[t])
    r21[t] = a2[t]
    wait_recv(5, r21.at[pl.ds(0, PLANE - 1)])
    r22[zh] = jnp.sum(r21[...], axis=0)
    send_all(6, column_high, NZH - 1, lambda j: r22.at[zh], r22.at[zh])
    wait_recv(6, r22.at[pl.ds(0, NZH - 1)])
    r23[t] = jnp.sum(r22[...], axis=0) / everyone
    send_all(7, block, PLANE - 1, lambda j: r23.at[t], r23.at[t])
    wait_recv(7, r23.at[pl.ds(0, PLANE - 1)])

    for a, out in enumerate((o_mid, o_feat)):
        for l in range(2):
            first = 32 * a + 16 * l
            out[:, 128 * l : 128 * l + 128] = r23[first : first + 16, 0:8, :].reshape(128, 128)
    for l in range(2):
        for s in range(32):
            o_out[4 * s : 4 * s + 4, 128 * l : 128 * l + 128] = r23[32 * l + s, 8:12, :]
    for l in range(2):
        o_gain[:, 128 * l : 128 * l + 128] = r23[l, 12:13, :]
        o_bias[:, 128 * l : 128 * l + 128] = r23[2 + l, 12:13, :]
    lane = iota((1, 128), 1)
    d_temper = jnp.zeros((1, 128), F32)
    for g in range(4):
        row = r23[4 + g, 12:13, :]
        for s in range(2):
            part = jnp.sum(jnp.where(lane // SLICES == s, row, 0.0), axis=1, keepdims=True)
            d_temper = jnp.where(lane == 2 * g + s, -part / temper[2 * g + s], d_temper)
    o_temper[...] = d_temper
    folded = jnp.concatenate([r23[8 + d, 12:13, :] for d in range(DIM)], axis=0)
    o_slice[...] = (folded + pltpu.roll(folded, SLICES, 1))[:, :SLICES]

    wait_send(0, r10)
    wait_send(1, r11.at[pl.ds(0, NXY - 1)])
    wait_send(2, r12.at[pl.ds(0, NZ - 1)])
    wait_send(3, r13.at[pl.ds(0, NXY * NC - 1)])
    wait_send(4, r20)
    wait_send(5, r21.at[pl.ds(0, PLANE - 1)])
    wait_send(6, r22.at[pl.ds(0, NZH - 1)])
    wait_send(7, r23.at[pl.ds(0, PLANE - 1)])


def shards(
    points, out_grad, ln_gain, ln_bias, w_mid, w_feat, w_slice, temper, wq, wk, wv, w_out
):
    rows = points.shape[0]
    everyone = rows * NXY * NZ * NC
    vmem = pl.BlockSpec(memory_space=pltpu.VMEM)
    smem = pl.BlockSpec(memory_space=pltpu.SMEM)
    f = lambda *s: jax.ShapeDtypeStruct(s, F32)
    outs = pl.pallas_call(
        functools.partial(kernel, float(everyone), 128),
        out_shape=(
            jax.ShapeDtypeStruct((rows, WIDTH), BF16),
            f(1, WIDTH),
            f(1, WIDTH),
            f(128, WIDTH),
            f(128, WIDTH),
            f(DIM, SLICES),
            f(1, 128),
            f(DIM, DIM),
            f(DIM, DIM),
            f(DIM, DIM),
            f(128, WIDTH),
        ),
        in_specs=[vmem] * 7 + [smem] + [vmem] * 4,
        out_specs=(vmem,) * 11,
        scratch_shapes=[
            pltpu.VMEM((rows, WIDTH), F32),
            pltpu.VMEM((rows, 128), F32),
            pltpu.VMEM((rows, WIDTH), BF16),
            pltpu.VMEM((rows, WIDTH), BF16),
            pltpu.VMEM((rows, 2 * WIDTH), BF16),
            pltpu.VMEM((rows, WIDTH), BF16),
            pltpu.VMEM((rows, COLS), F32),
            pltpu.VMEM((rows, COLS), F32),
            pltpu.VMEM((rows, COLS), BF16),
            pltpu.VMEM((rows, COLS), BF16),
            pltpu.VMEM((rows, 2 * WIDTH), BF16),
            pltpu.VMEM((rows, 2 * WIDTH), BF16),
            pltpu.VMEM((NC, NXY, ROWS1, 128), F32),
            pltpu.VMEM((NXY, ROWS1, 128), F32),
            pltpu.VMEM((NXY, ROWS1, 128), F32),
            pltpu.VMEM((NXY, ROWS1, 128), F32),
            pltpu.VMEM((NZ, ROWS1, 128), F32),
            pltpu.VMEM((NC * NXY, ROWS1, 128), F32),
            pltpu.VMEM((NC, PLANE, ROWS2, 128), F32),
            pltpu.VMEM((PLANE, ROWS2, 128), F32),
            pltpu.VMEM((PLANE, ROWS2, 128), F32),
            pltpu.VMEM((PLANE, ROWS2, 128), F32),
            pltpu.VMEM((NZH, ROWS2, 128), F32),
            pltpu.VMEM((8, 128), F32),
            pltpu.VMEM((PLANE, ROWS2, 128), F32),
            pltpu.SemaphoreType.DMA((8,)),
            pltpu.SemaphoreType.DMA((8,)),
        ],
        compiler_params=pltpu.CompilerParams(
            collective_id=0, has_side_effects=True, vmem_limit_bytes=48 * 1024 * 1024
        ),
    )(
        points,
        out_grad,
        ln_gain.reshape(1, -1),
        ln_bias.reshape(1, -1),
        w_mid,
        w_feat,
        w_slice,
        temper,
        wq,
        wk,
        wv,
        w_out,
    )
    outs = list(outs)
    outs[1] = outs[1].reshape(-1)
    outs[2] = outs[2].reshape(-1)
    outs[6] = outs[6][0, :HEADS]
    return tuple(outs)


def solution(mesh):
    by_point, by_rep = P(("pts", "rep"), None), P("rep", None)
    in_specs = (by_point, by_point) + (P(),) * 10
    out_specs = (by_point, P(), P(), by_rep, by_rep, P(), P(), P(), P(), P(), by_rep)
    return jax.shard_map(shards, mesh=mesh, in_specs=in_specs, out_specs=out_specs, check_vma=False)
```

time: 992 us -> 91.3 us (0.09)
  the two profiles are of different devices: /device:TPU:1 before, /device:TPU:4 now
where the time goes in v1:
time: 91.3 us; the launch traced here: 90.8 us
  Pallas kernels  75.3 us (82%)
  local copies, waits for them, and re-layouts  14.9 us (16%)
    pallas_call x1, Pallas kernels, shards(): pl.pallas_call(functools.partial(kernel, float(everyone), 128), out_shape...  75.3 us
    unnamed x34, local copies, waits for them, and re-layouts  14.3 us

profile of v1, /device:TPU:4, one launch (start us, length us, event | category | flops | bytes accessed | tf_op | source)
XLA Modules:
  0.0 90.8 jit_solution(12596161890738176455)
XLA Ops:
  0.6 0.0 copy-start.10
  0.7 0.0 copy-start.9
  0.7 0.0 copy-start.11
  0.7 0.7 copy-done.10
  1.3 0.0 copy-done.9
  1.3 0.0 copy-done.11
  1.3 0.0 copy-start
  1.3 0.9 %copy-done = bf16[512,256]{1,0:T(8,128)(2,1)S(1)} copy-done((bf16[512,256]{1,0:T(8,128)(2,1)S(1)}, bf16[512,256]{1,0:T(8,128)(2,1)}, u32[]{:S(2)}) %copy-start) | copy-done | bytes 262168
  2.3 0.0 copy-start.1
  2.3 0.9 %copy-done.1 = bf16[512,256]{1,0:T(8,128)(2,1)S(1)} copy-done((bf16[512,256]{1,0:T(8,128)(2,1)S(1)}, bf16[512,256]{1,0:T(8,128)(2,1)}, u32[]{:S(2)}) %copy-start.1) | copy-done | bytes 262168
  3.2 0.0 copy-start.2
  3.3 0.9 copy-done.2
  4.2 0.0 copy-start.3
  4.2 0.9 copy-done.3
  5.1 0.0 copy-start.4
  5.1 0.9 copy-done.4
  6.0 0.0 copy-start.5
  6.0 0.7 copy-done.5
  6.7 0.0 copy-start.6
  6.7 0.7 copy-done.6
  7.4 0.0 copy-start.7
  7.4 0.7 copy-done.7
  8.1 0.0 copy-start.8
  8.1 0.7 copy-done.8
  8.8 75.3 %shard_map.203 = (bf16[512,256]{1,0:T(8,128)(2,1)S(1)}, f32[1,256]{1,0:T(1,128)S(1)}, f32[1,256]{1,0:T(1,128)S(1)}, f32[128,256]{1,0:T(8,128)S(1)}, f32[128,256]...) custom-call(bf16[512,256]{1,0:T(8,128)(2,1)S(1)} %copy-done, ...), custom_call_target="tpu_custom_call" | custom-call | tf_op jit(solution)/shard_map/pallas_call | solution.py:424
  84.1 0.5 slice_bitcast_fusion
  84.6 0.7 copy.33
  85.3 0.6 copy.34
  85.9 0.6 copy.35
  86.4 0.7 copy.36
  87.1 0.7 copy.37
  87.7 0.6 copy.38
  88.3 0.6 copy.39
  89.0 0.6 copy.40
  89.6 0.6 copy.41
  90.2 0.7 copy.42
Async XLA Ops:
  0.6 0.7 copy-start.10
  0.7 0.7 copy-start.9
  0.7 0.7 copy-start.11
  1.3 1.0 %copy-start = (bf16[512,256]{1,0:T(8,128)(2,1)S(1)}, bf16[512,256]{1,0:T(8,128)(2,1)}, u32[]{:S(2)}) copy-start(bf16[512,256]{1,0:T(8,128)(2,1)} %points.1) | copy-start | bytes 786436
  2.3 0.9 %copy-start.1 = (bf16[512,256]{1,0:T(8,128)(2,1)S(1)}, bf16[512,256]{1,0:T(8,128)(2,1)}, u32[]{:S(2)}) copy-start(bf16[512,256]{1,0:T(8,128)(2,1)} %out_grad.1) | copy-start | bytes 786436
  3.2 0.9 copy-start.2
  4.2 0.9 copy-start.3
  5.1 0.9 copy-start.4
  6.0 0.7 copy-start.5
  6.7 0.7 copy-start.6
  7.4 0.7 copy-start.7
  8.1 0.7 copy-start.8

commit v2 on v1

v2 whole, which is shorter than its diff:
```python
import functools

import jax
import jax.numpy as jnp
from jax import lax
from jax.experimental import pallas as pl
from jax.experimental.pallas import tpu as pltpu
from jax.sharding import PartitionSpec as P

MESH = pl.DeviceIdType.MESH
F32, BF16 = jnp.float32, jnp.bfloat16
HI = lax.Precision.HIGHEST

HEADS, SLICES, DIM = 8, 64, 32
WIDTH = HEADS * DIM
COLS = HEADS * SLICES
NX, NY, NZ, NC = 4, 4, 16, 2
NXY = NX * NY
LOW = 4
NZH = NZ // LOW
ROWS1, ROWS2 = 9, 19
SMALL = 40
VMEM_BYTES = 60 * 1024 * 1024
BF_MAX = 3.3895314e38


def dot(a, b, ca=1, cb=0, precision=None):
    return lax.dot_general(
        a, b, (((ca,), (cb,)), ((), ())), preferred_element_type=F32, precision=precision
    )


def iota(shape, dim):
    return lax.broadcasted_iota(jnp.int32, shape, dim)


def split(values):
    high = values.astype(BF16)
    return high, (values - high.astype(F32)).astype(BF16)


def group_sum(high, low, ones):
    parts = []
    for g in range(0, COLS, 256):
        parts.append(dot(high[:, g : g + 256], ones) + dot(low[:, g : g + 256], ones))
    return jnp.concatenate(parts, axis=1)


def block_diagonal(tile_t):
    whole = jnp.concatenate([tile_t] * HEADS, axis=0)
    own = iota((WIDTH, COLS), 0) // DIM == iota((WIDTH, COLS), 1) // SLICES
    return jnp.where(own, whole, 0.0)


def diagonal_rows(full):
    left = iota((DIM, 128), 1) < SLICES
    parts = []
    for g in range(HEADS // 2):
        cols = slice(128 * g, 128 * g + 128)
        parts.append(
            jnp.where(
                left,
                full[2 * DIM * g : 2 * DIM * g + DIM, cols],
                full[2 * DIM * g + DIM : 2 * DIM * g + 2 * DIM, cols],
            )
        )
    return parts


def token_step(totals, masses, d_mixed, wq, wk, wv):
    scale = DIM ** (-0.5)
    inv = 1.0 / (masses + 1e-05)
    tokens = totals * inv
    q = dot(wq, tokens, 0, 0, HI)
    k = dot(wk, tokens, 0, 0, HI)
    v = dot(wv, tokens, 0, 0, HI)
    same = iota((128, 128), 0) // SLICES == iota((128, 128), 1) // SLICES
    mixed, dq, dk, dv = [], [], [], []
    for g in range(HEADS // 2):
        cols = slice(128 * g, 128 * g + 128)
        qg, kg, vg, dmg = q[:, cols], k[:, cols], v[:, cols], d_mixed[:, cols]
        powers = jnp.where(same, jnp.exp(dot(qg, kg, 0, 0, HI) * scale), 0.0)
        att = powers / jnp.sum(powers, axis=1, keepdims=True)
        mixed.append(dot(vg, att, 1, 1, HI))
        dv.append(dot(dmg, att, 1, 0, HI))
        d_att = dot(dmg, vg, 0, 0, HI)
        d_scores = att * (d_att - jnp.sum(d_att * att, axis=1, keepdims=True)) * scale
        dq.append(dot(kg, d_scores, 1, 1, HI))
        dk.append(dot(qg, d_scores, 1, 0, HI))
    join = functools.partial(jnp.concatenate, axis=1)
    mixed, dq, dk, dv = join(mixed), join(dq), join(dk), join(dv)
    d_tokens = dot(wq, dq, 1, 0, HI) + dot(wk, dk, 1, 0, HI) + dot(wv, dv, 1, 0, HI)
    grads = [dot(tokens, d, 1, 1, HI) for d in (dq, dk, dv)]
    d_masses = -jnp.sum(d_tokens * tokens, axis=0, keepdims=True) * inv
    return mixed, d_tokens * inv, d_masses, grads


def far_first(a):
    return (2 - a + 3 * (a // 2) - 2 * (a // 3)) % 4


def kernel(
    everyone,
    chunk,
    points_h,
    out_grad_h,
    gain_h,
    bias_h,
    w_mid_h,
    w_feat_h,
    w_slice_h,
    temper_h,
    wq_h,
    wk_h,
    wv_h,
    w_out_h,
    h_points,
    h_gain,
    h_bias,
    h_mid,
    h_feat,
    h_slice,
    h_temper,
    h_q,
    h_k,
    h_v,
    h_out,
    o_points,
    o_gain,
    o_bias,
    o_mid,
    o_feat,
    o_slice,
    o_temper,
    o_q,
    o_k,
    o_v,
    o_out,
    stores,
    points,
    out_grad,
    gain_ref,
    bias_ref,
    w_mid,
    w_feat,
    w_slice,
    temper,
    wq,
    wk,
    wv,
    w_out,
    loads,
    xhat_s,
    rstd_s,
    normed_s,
    mid_s,
    fd_s,
    low_s,
    logits_s,
    w_s,
    sw_s,
    sc_s,
    dmf_s,
    ds_s,
    dn_s,
    p1,
    r10,
    a1,
    r11,
    r12,
    r13,
    pa,
    ra0,
    aa,
    ra1,
    ra2,
    ra3,
    ra4,
    ra5,
    pb,
    rb0,
    ab,
    rb1,
    rb2,
    rb3,
    sends,
    recvs,
):
    held = (
        (points_h, points),
        (w_mid_h, w_mid),
        (w_feat_h, w_feat),
        (gain_h, gain_ref),
        (bias_h, bias_ref),
        (w_slice_h, w_slice),
        (temper_h, temper),
        (out_grad_h, out_grad),
        (w_out_h, w_out),
        (wq_h, wq),
        (wk_h, wk),
        (wv_h, wv),
    )
    copies = [pltpu.make_async_copy(a, b, loads.at[n]) for n, (a, b) in enumerate(held)]
    for copy in copies:
        copy.start()

    p, c = lax.axis_index("pts"), lax.axis_index("rep")
    x, y, z = p // (NY * NZ), p // NZ % NY, p % NZ
    xy = x * NY + y
    zl, zh = z % LOW, z // LOW
    rows = points.shape[0]

    def plane_index(i):
        return (x + far_first(i // 4)) % NX * NY + (y + far_first(i % 4)) % NY

    def plane(i):
        return (plane_index(i) * NZ + z, c)

    def plane_cores(i):
        return (plane_index(i // 2) * NZ + z, (c + 1 + i % 2) % NC)

    def column(i):
        return (xy * NZ + (z + 8 + (i + 1) // 2 * (1 - 2 * (i % 2))) % NZ, c)

    def low_index(i):
        return (zl + far_first(i)) % LOW

    def column_low(i):
        return (xy * NZ + zh * LOW + low_index(i), c)

    def column_high(i):
        return (xy * NZ + (z + LOW * far_first(i)) % NZ, c)

    sibling = (p, 1 - c)
    made = (
        (o_points, h_points),
        (o_gain, h_gain),
        (o_bias, h_bias),
        (o_mid, h_mid),
        (o_feat, h_feat),
        (o_slice, h_slice),
        (o_temper, h_temper),
        (o_q, h_q),
        (o_k, h_k),
        (o_v, h_v),
        (o_out, h_out),
    )
    writes = [pltpu.make_async_copy(a, b, stores.at[n]) for n, (a, b) in enumerate(made)]

    barrier = pltpu.get_barrier_semaphore()

    def greet(who, count):
        def body(i, _):
            pl.semaphore_signal(barrier, inc=1, device_id=who(i), device_id_type=MESH)
            return 0

        lax.fori_loop(0, count, body, 0)

    with jax.named_scope("greet"):
        greet(plane_cores, 2 * NXY - 1)
        greet(column, NZ - 1)

    unsent, started = [], []

    def send_all(stage, who, count, src, dst):
        def body(i, _):
            pltpu.make_async_remote_copy(
                src(i), dst, sends.at[stage], recvs.at[stage], device_id=who(i), device_id_type=MESH
            ).start()
            return 0

        lax.fori_loop(0, count, body, 0)

    def swap(stage, src, dst):
        send_all(stage, lambda i: sibling, 1, lambda i: src, dst)

    def wait(stage, ref):
        copy = pltpu.make_async_remote_copy(
            ref, ref, sends.at[stage], recvs.at[stage], device_id=sibling, device_id_type=MESH
        )
        copy.wait_recv()
        unsent.append(copy)

    def write(n):
        writes[n].start()
        started.append(writes[n])

    ones = (iota((256, 256), 0) // SLICES == iota((256, 256), 1) // SLICES).astype(F32).astype(BF16)

    with jax.named_scope("load"):
        for copy in copies:
            copy.wait()
    gain, bias = gain_ref[...], bias_ref[...]
    head_of = iota((1, COLS), 1) // SLICES
    temper_row = jnp.zeros((1, COLS), F32)
    for h in range(HEADS):
        temper_row = jnp.where(head_of == h, temper[:, h : h + 1], temper_row)
    inv_t = 1.0 / temper_row
    ws = w_slice[...].astype(F32)
    slice_blocks = block_diagonal(jnp.concatenate([ws] * HEADS, axis=1)).astype(BF16)

    with jax.named_scope("front"):
        for r in range(0, rows, chunk):
            here = pl.ds(r, chunk)
            xs = points[here, :].astype(F32)
            center = xs - jnp.mean(xs, axis=1, keepdims=True)
            rstd = lax.rsqrt(jnp.mean(center * center, axis=1, keepdims=True) + 1e-05)
            xhat = center * rstd
            xhat_s[here, :] = xhat
            rstd_s[here, :] = jnp.broadcast_to(rstd, (chunk, 128))
            normed = (xhat * gain + bias).astype(BF16)
            normed_s[here, :] = normed
            mid = dot(normed, w_mid[...]).astype(BF16)
            mid_s[here, :] = mid
            fd_s[here, WIDTH:] = dot(normed, w_feat[...]).astype(BF16)
            logits = dot(mid, slice_blocks) * inv_t
            logits_s[here, :] = logits
            powers = jnp.exp(logits)
            high = jnp.minimum(powers, BF_MAX).astype(BF16)
            low = (powers - high.astype(F32)).astype(BF16)
            weights = powers / group_sum(high, low, ones)
            w_s[here, :] = weights
            sw_s[here, :] = weights.astype(BF16)
            d_high, d_low = split(dot(out_grad[here, :], w_out[...], 1, 1))
            fd_s[here, :WIDTH] = d_high
            low_s[here, :] = d_low

    with jax.named_scope("shares1"):
        sw = sw_s[...]
        by_fd = dot(fd_s[...], sw, 0, 0)
        by_low = dot(low_s[...], sw, 0, 0)
        tot = diagonal_rows(by_fd[WIDTH:])
        dmx = diagonal_rows(by_fd[:WIDTH] + by_low)
        mass = dot(jnp.ones((8, rows), BF16), sw)[:1]
        quarter = iota((1, 128), 1) // DIM
        for i in range(4):
            for j in range(4):
                k = 4 * i + j
                p1[0, k, 0:8, :] = tot[j][8 * i : 8 * i + 8]
                p1[1, k, 0:8, :] = dmx[j][8 * i : 8 * i + 8]
                p1[0, k, 8:9, :] = jnp.where(quarter == i, mass[:, 128 * j : 128 * j + 128], 0.0)
                p1[1, k, 8:9, :] = jnp.zeros((1, 128), F32)

    with jax.named_scope("barrier"):
        pl.semaphore_wait(barrier, 2 * NXY - 1 + NZ - 1)

    with jax.named_scope("sum1_core"):
        swap(0, p1.at[1 - c], r10)
        wait(0, r10)
        a1[...] = p1[c] + r10[...]
    with jax.named_scope("sum1_plane"):
        send_all(1, plane, NXY - 1, lambda i: a1.at[plane_index(i)], r11.at[xy])
        r11[xy] = a1[xy]
        wait(1, r11.at[pl.ds(0, NXY - 1)])
        r12[z] = jnp.sum(r11[...], axis=0)
    with jax.named_scope("sum1_column"):
        send_all(2, column, NZ - 1, lambda i: r12.at[z], r12.at[z])
        wait(2, r12.at[pl.ds(0, NZ - 1)])
        me1 = c * NXY + xy
        r13[me1] = jnp.sum(r12[...], axis=0)
    with jax.named_scope("sum1_back"):
        send_all(3, plane_cores, 2 * NXY - 1, lambda i: r13.at[me1], r13.at[me1])
        wait(3, r13.at[pl.ds(0, 2 * NXY - 1)])

    def whole(half):
        return jnp.concatenate(
            [
                jnp.concatenate([r13[NXY * half + 4 * i + j, 0:8, :] for i in range(4)], axis=0)
                for j in range(4)
            ],
            axis=1,
        )

    with jax.named_scope("tokens"):
        masses = jnp.concatenate(
            [sum(r13[4 * i + j, 8:9, :] for i in range(4)) for j in range(4)], axis=1
        )
        mixed, d_totals, d_masses, grads = token_step(
            whole(0), masses, whole(1), wq[...], wk[...], wv[...]
        )
        for out, grad in zip((o_q, o_k, o_v), grads):
            out[...] = grad / everyone
        for n in (7, 8, 9):
            write(n)
        both = jnp.concatenate(
            [
                block_diagonal(mixed.astype(BF16).astype(F32)).astype(BF16),
                block_diagonal(d_totals.astype(BF16).astype(F32)).astype(BF16),
            ],
            axis=0,
        )

    with jax.named_scope("feat_out"):
        for r in range(0, rows, chunk):
            here = pl.ds(r, chunk)
            by_both = dot(sw_s[here, :], both, 1, 1)
            dmf_s[here, WIDTH:] = by_both[:, WIDTH:].astype(BF16)
            s_high, s_low = split(by_both[:, :WIDTH])
            ds_s[here, :WIDTH] = s_high
            ds_s[here, WIDTH:] = s_low
        by_normed = dot(normed_s[...], dmf_s[:, WIDTH:], 0, 0)
        by_slices = dot(ds_s[...], out_grad[...], 0, 0)
        out_w = by_slices[:WIDTH] + by_slices[WIDTH:]
        for h in range(NC):
            half = slice(128 * h, 128 * h + 128)
            for a, grad in enumerate((by_normed, out_w)):
                for l in range(2):
                    first = 8 * a + 4 * l
                    pa[h, first : first + 4] = grad[half, 128 * l : 128 * l + 128].reshape(
                        4, LOW, 8, 128
                    )
        swap(4, pa.at[1 - c], ra0)

    w_both = jnp.concatenate([w_mid[...], w_feat[...]], axis=1)

    def fold(values):
        return jnp.sum(values.reshape(values.shape[0] // 8, 8, values.shape[1]), axis=0)

    sums = [jnp.zeros((8, COLS), F32), jnp.zeros((8, WIDTH), F32), jnp.zeros((8, WIDTH), F32)]

    def back(r):
        here = pl.ds(r, chunk)
        weights = w_s[here, :]
        d_weights = dot(fd_s[here, :], both) + d_masses
        high, low = split(d_weights * weights)
        d_logits = weights * (d_weights - group_sum(high, low, ones))
        scaled = (d_logits * inv_t).astype(BF16)
        sc_s[here, :] = scaled
        sums[0] += fold(d_logits * logits_s[here, :])
        dmf_s[here, :WIDTH] = dot(scaled, slice_blocks, 1, 1).astype(BF16)
        d_normed = dot(dmf_s[here, :], w_both, 1, 1)
        dn_s[here, :] = d_normed
        sums[1] += fold(d_normed * xhat_s[here, :])
        sums[2] += fold(d_normed)

    with jax.named_scope("back_first"):
        for r in range(0, rows // 2, chunk):
            back(r)
    with jax.named_scope("suma_core"):
        wait(4, ra0)
        aa[...] = pa[c] + ra0[...]
        send_all(5, plane, NXY - 1, lambda i: aa.at[plane_index(i)], ra1.at[xy])
        ra1[xy] = aa[xy]
    with jax.named_scope("back_second"):
        for r in range(rows // 2, rows, chunk):
            back(r)
    with jax.named_scope("sharesb"):
        grad_mid = dot(normed_s[...], dmf_s[:, :WIDTH], 0, 0)
        slice_sum = sum(diagonal_rows(dot(mid_s[...], sc_s[...], 0, 0)))
        temper_sum, gain_sum, bias_sum = (jnp.sum(v, axis=0, keepdims=True) for v in sums)
        small = [gain_sum[:, 128 * l : 128 * l + 128] for l in range(2)]
        small += [bias_sum[:, 128 * l : 128 * l + 128] for l in range(2)]
        small += [temper_sum[:, 128 * l : 128 * l + 128] for l in range(4)]
        small += [slice_sum[d : d + 1] for d in range(DIM)]
        small += [jnp.zeros((1, 128), F32)] * (3 * NXY - len(small))
        small = jnp.concatenate(small, axis=0)
        for h in range(NC):
            for l in range(2):
                pb[h, 8 * l : 8 * l + 8, 0:16, :] = grad_mid[
                    128 * h : 128 * h + 128, 128 * l : 128 * l + 128
                ].reshape(8, 16, 128)
            for k in range(NXY):
                pb[h, k, 16:19, :] = small[3 * k : 3 * k + 3]

    with jax.named_scope("sumb_core"):
        swap(9, pb.at[1 - c], rb0)
    with jax.named_scope("suma_plane"):
        wait(5, ra1.at[pl.ds(0, NXY - 1)])
        ra2[...] = jnp.sum(ra1[...], axis=0)
        send_all(6, column_low, LOW - 1, lambda i: ra2.at[low_index(i)], ra3.at[zl])
        ra3[zl] = ra2[zl]
    with jax.named_scope("sumb_plane"):
        wait(9, rb0)
        ab[...] = pb[c] + rb0[...]
        send_all(10, plane, NXY - 1, lambda i: ab.at[plane_index(i)], rb1.at[xy])
        rb1[xy] = ab[xy]

    with jax.named_scope("points"):
        for r in range(0, rows, chunk):
            here = pl.ds(r, chunk)
            xhat = xhat_s[here, :]
            d_xhat = dn_s[here, :] * gain
            inner = d_xhat - jnp.mean(d_xhat, axis=1, keepdims=True)
            inner = inner - xhat * jnp.mean(d_xhat * xhat, axis=1, keepdims=True)
            o_points[here, :] = (inner * rstd_s[here, 0:1]).astype(BF16)
        write(0)

    with jax.named_scope("suma_low"):
        wait(6, ra3.at[pl.ds(0, LOW - 1)])
        ra4[zh] = jnp.sum(ra3[...], axis=0)
        send_all(7, column_high, NZH - 1, lambda i: ra4.at[zh], ra4.at[zh])
    with jax.named_scope("sumb_column"):
        wait(10, rb1.at[pl.ds(0, NXY - 1)])
        rb2[z] = jnp.sum(rb1[...], axis=0)
        send_all(11, column, NZ - 1, lambda i: rb2.at[z], rb2.at[z])
    with jax.named_scope("suma_high"):
        wait(7, ra4.at[pl.ds(0, NZH - 1)])
        ra5[xy, zl] = jnp.sum(ra4[...], axis=0) / everyone
        send_all(8, column_low, LOW - 1, lambda i: ra5.at[xy, zl], ra5.at[xy, zl])
        wait(8, ra5.at[xy, pl.ds(0, LOW - 1)])
        send_all(12, plane, NXY - 1, lambda i: ra5.at[xy], ra5.at[xy])
    with jax.named_scope("sumb_back"):
        wait(11, rb2.at[pl.ds(0, NZ - 1)])
        rb3[xy] = jnp.sum(rb2[...], axis=0) / everyone
        send_all(13, plane, NXY - 1, lambda i: rb3.at[xy], rb3.at[xy])
    with jax.named_scope("suma_last"):
        wait(12, ra5.at[pl.ds(0, NXY - 1)])
        for a, out in enumerate((o_feat, o_out)):
            for l in range(2):
                first = 8 * a + 4 * l
                out[:, 128 * l : 128 * l + 128] = ra5[first : first + 4].reshape(128, 128)
        write(4)
        write(10)
    with jax.named_scope("sumb_last"):
        wait(13, rb3.at[pl.ds(0, NXY - 1)])
        for l in range(2):
            o_mid[:, 128 * l : 128 * l + 128] = rb3[8 * l : 8 * l + 8, 0:16, :].reshape(128, 128)
        small = [rb3[k // 3, 16 + k % 3 : 17 + k % 3, :] for k in range(SMALL)]
        for l in range(2):
            o_gain[:, 128 * l : 128 * l + 128] = small[l]
            o_bias[:, 128 * l : 128 * l + 128] = small[2 + l]
        folded = jnp.concatenate(small[8:], axis=0)
        o_slice[...] = (folded + pltpu.roll(folded, SLICES, 1))[:, :SLICES]
        lane, place = iota((1, 128), 1), iota((1, HEADS), 1)
        d_temper = jnp.zeros((1, HEADS), F32)
        for g in range(4):
            for s in range(2):
                part = jnp.where(lane // SLICES == s, small[4 + g], 0.0)
                part = jnp.sum(part, axis=1, keepdims=True)
                d_temper = jnp.where(place == 2 * g + s, part, d_temper)
        o_temper[...] = -d_temper / temper[...]
        for n in (1, 2, 3, 5, 6):
            write(n)

    with jax.named_scope("done"):
        for copy in unsent:
            copy.wait_send()
        for copy in started:
            copy.wait()


def hand_on(count, *refs):
    ins, outs, held, (loads, stores) = (
        refs[:count],
        refs[count : 2 * count],
        refs[2 * count : 3 * count],
        refs[3 * count :],
    )
    one = [pltpu.make_async_copy(ins[n], held[n], loads.at[n]) for n in range(count)]
    two = [pltpu.make_async_copy(held[n], outs[n], stores.at[n]) for n in range(count)]
    for copy in one:
        copy.start()
    for first, second in zip(one, two):
        first.wait()
        second.start()
    for copy in two:
        copy.wait()


def shards(
    points, out_grad, ln_gain, ln_bias, w_mid, w_feat, w_slice, temper, wq, wk, wv, w_out
):
    rows = points.shape[0]
    everyone = rows * NXY * NZ * NC
    hbm = pl.BlockSpec(memory_space=pltpu.HBM)
    f = lambda *s: jax.ShapeDtypeStruct(s, F32)
    args = (
        points,
        out_grad,
        ln_gain.reshape(1, -1),
        ln_bias.reshape(1, -1),
        w_mid,
        w_feat,
        w_slice,
        temper.reshape(1, -1),
        wq,
        wk,
        wv,
        w_out,
    )
    out_shape = (
        jax.ShapeDtypeStruct((rows, WIDTH), BF16),
        f(1, WIDTH),
        f(1, WIDTH),
        f(128, WIDTH),
        f(128, WIDTH),
        f(DIM, SLICES),
        f(1, HEADS),
        f(DIM, DIM),
        f(DIM, DIM),
        f(DIM, DIM),
        f(128, WIDTH),
    )
    outs = pl.pallas_call(
        functools.partial(kernel, float(everyone), 128),
        out_shape=out_shape,
        in_specs=[hbm] * 12,
        out_specs=(hbm,) * 11,
        scratch_shapes=[pltpu.VMEM(a.shape, a.dtype) for a in out_shape]
        + [pltpu.SemaphoreType.DMA((11,))]
        + [pltpu.VMEM(a.shape, a.dtype) for a in args]
        + [pltpu.SemaphoreType.DMA((12,))]
        + [
            pltpu.VMEM((rows, WIDTH), F32),
            pltpu.VMEM((rows, 128), F32),
            pltpu.VMEM((rows, WIDTH), BF16),
            pltpu.VMEM((rows, WIDTH), BF16),
            pltpu.VMEM((rows, 2 * WIDTH), BF16),
            pltpu.VMEM((rows, WIDTH), BF16),
            pltpu.VMEM((rows, COLS), F32),
            pltpu.VMEM((rows, COLS), F32),
            pltpu.VMEM((rows, COLS), BF16),
            pltpu.VMEM((rows, COLS), BF16),
            pltpu.VMEM((rows, 2 * WIDTH), BF16),
            pltpu.VMEM((rows, 2 * WIDTH), BF16),
            pltpu.VMEM((rows, WIDTH), F32),
        ]
        + [
            pltpu.VMEM(lead + (ROWS1, 128), F32)
            for lead in ((NC, NXY), (NXY,), (NXY,), (NXY,), (NZ,), (NC * NXY,))
        ]
        + [
            pltpu.VMEM(lead + (8, 128), F32)
            for lead in (
                (NC, NXY, LOW),
                (NXY, LOW),
                (NXY, LOW),
                (NXY, LOW),
                (LOW,),
                (LOW,),
                (NZH,),
                (NXY, LOW),
            )
        ]
        + [
            pltpu.VMEM(lead + (ROWS2, 128), F32)
            for lead in ((NC, NXY), (NXY,), (NXY,), (NXY,), (NZ,), (NXY,))
        ]
        + [pltpu.SemaphoreType.DMA((14,)), pltpu.SemaphoreType.DMA((14,))],
        compiler_params=pltpu.CompilerParams(
            collective_id=0, has_side_effects=True, vmem_limit_bytes=VMEM_BYTES
        ),
        name="backward",
    )(*args)
    outs = pl.pallas_call(
        functools.partial(hand_on, len(outs)),
        out_shape=out_shape,
        in_specs=[hbm] * 11,
        out_specs=(hbm,) * 11,
        scratch_shapes=[pltpu.VMEM(a.shape, a.dtype) for a in out_shape]
        + [pltpu.SemaphoreType.DMA((11,))] * 2,
        compiler_params=pltpu.CompilerParams(vmem_limit_bytes=VMEM_BYTES),
        name="hand_on",
    )(*outs)
    outs = list(outs)
    for n in (1, 2, 6):
        outs[n] = outs[n].reshape(-1)
    return tuple(outs)


def solution(mesh):
    by_point, by_rep = P(("pts", "rep"), None), P("rep", None)
    in_specs = (by_point, by_point) + (P(),) * 10
    out_specs = (by_point, P(), P(), by_rep, by_rep, P(), P(), P(), P(), P(), by_rep)
    return jax.shard_map(shards, mesh=mesh, in_specs=in_specs, out_specs=out_specs, check_vma=False)
```

time: 91.3 us -> 74.3 us (0.81)
  the two profiles are of different devices: /device:TPU:4 before, /device:TPU:2 now
where the time goes in v2:
time: 74.3 us; the launch traced here: 74.2 us
  Pallas kernels  73.5 us (99%)
    pallas_call x1, Pallas kernels, shards(): pl.pallas_call(functools.partial(kernel, float(everyone), 128), out_shape...  71.5 us
    pallas_call x1, Pallas kernels, shards(): pl.pallas_call(functools.partial(hand_on, len(outs)), out_shape=out_shape...  2.02 us

profile of v2, /device:TPU:2, one launch (start us, length us, event | category | flops | bytes accessed | tf_op | source)
XLA Modules:
  0.0 74.2 jit_solution(17528844148518224410)
XLA Ops:
  0.6 71.5 %backward.1 = (bf16[512,256]{1,0:T(8,128)(2,1)}, f32[1,256]{1,0:T(1,128)}, f32[1,256]{1,0:T(1,128)}, f32[128,256]{1,0:T(8,128)}, f32[128,256]{1,0:T(8,128)}, /*i...) custom-call(bf16[512,256]{1,0:T(8,128)(2,1)} %points_h.1, ...), custom_call_target="tpu_custom_call" | custom-call | tf_op jit(solution)/shard_map/backward/pallas_call | solution.py:594
  72.2 2.0 %hand_on.1 = (bf16[512,256]{1,0:T(8,128)(2,1)}, f32[1,256]{1,0:T(1,128)}, f32[1,256]{1,0:T(1,128)}, f32[128,256]{1,0:T(8,128)}, f32[128,256]{1,0:T(8,128)}, /*in...) custom-call(bf16[512,256]{1,0:T(8,128)(2,1)} %get-tuple-element.33.r, ...), custom_call_target="tpu_custom_call" | custom-call | tf_op jit(solution)/shard_map/hand_on/pallas_call | solution.py:645

commit v3 on v2

--- a/solution.py
+++ b/solution.py
@@ -67,32 +67,62 @@
     return parts
 
 
-def token_step(totals, masses, d_mixed, wq, wk, wv):
+def thirds(values):
+    first = values.astype(BF16)
+    rest = values - first.astype(F32)
+    second = rest.astype(BF16)
+    return first, second, (rest - second.astype(F32)).astype(BF16)
+
+
+def left_terms(parts, axis=0):
+    a, b, c = parts
+    return jnp.concatenate([a, a, b, a, b, c], axis=axis)
+
+
+def right_terms(parts, axis=0):
+    a, b, c = parts
+    return jnp.concatenate([a, b, a, c, b, a], axis=axis)
+
+
+def weight_terms(weights):
+    terms = [part.astype(F32) for part in thirds(weights)]
+    return left_terms(terms, 1).astype(BF16)
+
+
+def pair_dot(left, right, cb):
+    a, b = split(left)
+    c, d = split(right)
+    return dot(jnp.concatenate([a, a, b], axis=1), jnp.concatenate([c, d, c], axis=cb), 1, cb)
+
+
+def token_step(totals, masses, d_mixed, forward_terms, backward_terms):
     scale = DIM ** (-0.5)
     inv = 1.0 / (masses + 1e-05)
     tokens = totals * inv
-    q = dot(wq, tokens, 0, 0, HI)
-    k = dot(wk, tokens, 0, 0, HI)
-    v = dot(wv, tokens, 0, 0, HI)
+    qkv = dot(forward_terms, right_terms(thirds(tokens)))
+    q, k, v = qkv[:DIM], qkv[DIM : 2 * DIM], qkv[2 * DIM :]
+    q_terms, k_terms = left_terms(thirds(q)), right_terms(thirds(k))
+    m_terms, v_terms = left_terms(thirds(d_mixed)), right_terms(thirds(v))
     same = iota((128, 128), 0) // SLICES == iota((128, 128), 1) // SLICES
     mixed, dq, dk, dv = [], [], [], []
     for g in range(HEADS // 2):
         cols = slice(128 * g, 128 * g + 128)
-        qg, kg, vg, dmg = q[:, cols], k[:, cols], v[:, cols], d_mixed[:, cols]
-        powers = jnp.where(same, jnp.exp(dot(qg, kg, 0, 0, HI) * scale), 0.0)
+        scores = dot(q_terms[:, cols], k_terms[:, cols], 0, 0) * scale
+        d_att = dot(m_terms[:, cols], v_terms[:, cols], 0, 0)
+        powers = jnp.where(same, jnp.exp(scores), 0.0)
         att = powers / jnp.sum(powers, axis=1, keepdims=True)
-        mixed.append(dot(vg, att, 1, 1, HI))
-        dv.append(dot(dmg, att, 1, 0, HI))
-        d_att = dot(dmg, vg, 0, 0, HI)
         d_scores = att * (d_att - jnp.sum(d_att * att, axis=1, keepdims=True)) * scale
-        dq.append(dot(kg, d_scores, 1, 1, HI))
-        dk.append(dot(qg, d_scores, 1, 0, HI))
-    join = functools.partial(jnp.concatenate, axis=1)
-    mixed, dq, dk, dv = join(mixed), join(dq), join(dk), join(dv)
-    d_tokens = dot(wq, dq, 1, 0, HI) + dot(wk, dk, 1, 0, HI) + dot(wv, dv, 1, 0, HI)
-    grads = [dot(tokens, d, 1, 1, HI) for d in (dq, dk, dv)]
+        mixed.append(pair_dot(v[:, cols], att, 1))
+        dq.append(pair_dot(k[:, cols], d_scores, 1))
+        dk.append(pair_dot(q[:, cols], d_scores, 0))
+        dv.append(pair_dot(d_mixed[:, cols], att, 0))
+    mixed = jnp.concatenate(mixed, axis=1)
+    backs = [jnp.concatenate(d, axis=1) for d in (dq, dk, dv)]
+    d_tokens = dot(
+        backward_terms, jnp.concatenate([right_terms(thirds(d)) for d in backs], axis=0)
+    )
     d_masses = -jnp.sum(d_tokens * tokens, axis=0, keepdims=True) * inv
-    return mixed, d_tokens * inv, d_masses, grads
+    return mixed, d_tokens * inv, d_masses, tokens, backs
 
 
 def far_first(a):
@@ -161,7 +191,6 @@
     sw_s,
     sc_s,
     dmf_s,
-    ds_s,
     dn_s,
     p1,
     r10,
@@ -176,13 +205,21 @@
     ra2,
     ra3,
     ra4,
-    ra5,
     pb,
     rb0,
     ab,
     rb1,
     rb2,
     rb3,
+    pp,
+    rp0,
+    ap,
+    rp1,
+    sp,
+    rp2,
+    rp3,
+    rp4,
+    mb_s,
     sends,
     recvs,
 ):
@@ -219,8 +256,11 @@
     def plane_cores(i):
         return (plane_index(i // 2) * NZ + z, (c + 1 + i % 2) % NC)
 
+    def column_index(i):
+        return (z + 8 + (i + 1) // 2 * (1 - 2 * (i % 2))) % NZ
+
     def column(i):
-        return (xy * NZ + (z + 8 + (i + 1) // 2 * (1 - 2 * (i % 2))) % NZ, c)
+        return (xy * NZ + column_index(i), c)
 
     def low_index(i):
         return (zl + far_first(i)) % LOW
@@ -249,18 +289,27 @@
 
     barrier = pltpu.get_barrier_semaphore()
 
-    def greet(who, count):
-        def body(i, _):
+    greetings = [(plane_cores, i) for i in range(2 * NXY - 1)]
+    greetings += [(column, i) for i in range(NZ - 1)]
+    n_greetings = len(greetings)
+
+    def greet(count):
+        for who, i in greetings[:count]:
             pl.semaphore_signal(barrier, inc=1, device_id=who(i), device_id_type=MESH)
-            return 0
-
-        lax.fori_loop(0, count, body, 0)
-
-    with jax.named_scope("greet"):
-        greet(plane_cores, 2 * NXY - 1)
-        greet(column, NZ - 1)
+        del greetings[:count]
 
     unsent, started = [], []
+
+    def pack(ref, grad):
+        for h in range(NC):
+            for l in range(2):
+                ref[h, 8 * l : 8 * l + 8, 0:16, :] = grad[
+                    128 * h : 128 * h + 128, 128 * l : 128 * l + 128
+                ].reshape(8, 16, 128)
+
+    def unpack(ref, out):
+        for l in range(2):
+            out[:, 128 * l : 128 * l + 128] = ref[8 * l : 8 * l + 8, 0:16, :].reshape(128, 128)
 
     def send_all(stage, who, count, src, dst):
         def body(i, _):
@@ -288,7 +337,7 @@
     ones = (iota((256, 256), 0) // SLICES == iota((256, 256), 1) // SLICES).astype(F32).astype(BF16)
 
     with jax.named_scope("load"):
-        for copy in copies:
+        for copy in copies[:7]:
             copy.wait()
     gain, bias = gain_ref[...], bias_ref[...]
     head_of = iota((1, COLS), 1) // SLICES
@@ -302,6 +351,7 @@
     with jax.named_scope("front"):
         for r in range(0, rows, chunk):
             here = pl.ds(r, chunk)
+            greet(-(-n_greetings * chunk // rows))
             xs = points[here, :].astype(F32)
             center = xs - jnp.mean(xs, axis=1, keepdims=True)
             rstd = lax.rsqrt(jnp.mean(center * center, axis=1, keepdims=True) + 1e-05)
@@ -321,6 +371,10 @@
             weights = powers / group_sum(high, low, ones)
             w_s[here, :] = weights
             sw_s[here, :] = weights.astype(BF16)
+        for copy in copies[7:]:
+            copy.wait()
+        for r in range(0, rows, chunk):
+            here = pl.ds(r, chunk)
             d_high, d_low = split(dot(out_grad[here, :], w_out[...], 1, 1))
             fd_s[here, :WIDTH] = d_high
             low_s[here, :] = d_low
@@ -342,24 +396,42 @@
                 p1[1, k, 8:9, :] = jnp.zeros((1, 128), F32)
 
     with jax.named_scope("barrier"):
-        pl.semaphore_wait(barrier, 2 * NXY - 1 + NZ - 1)
+        pl.semaphore_wait(barrier, n_greetings)
 
     with jax.named_scope("sum1_core"):
         swap(0, p1.at[1 - c], r10)
+        token_weights = (wq[...], wk[...], wv[...])
+        forward_terms = jnp.concatenate([weight_terms(w.T) for w in token_weights], axis=0)
+        backward_terms = jnp.concatenate([weight_terms(w) for w in token_weights], axis=1)
+        projected = dot(out_grad[...], sw, 0, 0)
+        for h in range(NC):
+            half = projected[:, WIDTH * h : WIDTH * h + WIDTH]
+            pp[h] = half.reshape(NXY, 16, WIDTH)
         wait(0, r10)
         a1[...] = p1[c] + r10[...]
     with jax.named_scope("sum1_plane"):
         send_all(1, plane, NXY - 1, lambda i: a1.at[plane_index(i)], r11.at[xy])
+        swap(13, pp.at[1 - c], rp0)
         r11[xy] = a1[xy]
         wait(1, r11.at[pl.ds(0, NXY - 1)])
         r12[z] = jnp.sum(r11[...], axis=0)
     with jax.named_scope("sum1_column"):
         send_all(2, column, NZ - 1, lambda i: r12.at[z], r12.at[z])
+        wait(13, rp0)
+        ap[...] = pp[c] + rp0[...]
+        send_all(14, plane, NXY - 1, lambda i: ap.at[plane_index(i)], rp1.at[xy])
+        rp1[xy] = ap[xy]
         wait(2, r12.at[pl.ds(0, NZ - 1)])
         me1 = c * NXY + xy
         r13[me1] = jnp.sum(r12[...], axis=0)
     with jax.named_scope("sum1_back"):
         send_all(3, plane_cores, 2 * NXY - 1, lambda i: r13.at[me1], r13.at[me1])
+        wait(14, rp1.at[pl.ds(0, NXY - 1)])
+        piece = jnp.sum(rp1[...], axis=0)
+        for k in range(NZ):
+            sp[k] = piece[k : k + 1]
+        send_all(15, column, NZ - 1, lambda i: sp.at[column_index(i)], rp2.at[z])
+        rp2[z] = sp[z]
         wait(3, r13.at[pl.ds(0, 2 * NXY - 1)])
 
     def whole(half):
@@ -375,41 +447,28 @@
         masses = jnp.concatenate(
             [sum(r13[4 * i + j, 8:9, :] for i in range(4)) for j in range(4)], axis=1
         )
-        mixed, d_totals, d_masses, grads = token_step(
-            whole(0), masses, whole(1), wq[...], wk[...], wv[...]
+        mixed, d_totals, d_masses, tokens, backs = token_step(
+            whole(0), masses, whole(1), forward_terms, backward_terms
         )
-        for out, grad in zip((o_q, o_k, o_v), grads):
-            out[...] = grad / everyone
-        for n in (7, 8, 9):
-            write(n)
-        both = jnp.concatenate(
-            [
-                block_diagonal(mixed.astype(BF16).astype(F32)).astype(BF16),
-                block_diagonal(d_totals.astype(BF16).astype(F32)).astype(BF16),
-            ],
-            axis=0,
-        )
-
-    with jax.named_scope("feat_out"):
+        mixed_blocks = block_diagonal(mixed.astype(BF16).astype(F32)).astype(BF16)
+        totals_blocks = block_diagonal(d_totals.astype(BF16).astype(F32)).astype(BF16)
+        both = jnp.concatenate([mixed_blocks, totals_blocks], axis=0)
+        for h in range(NC):
+            mb_s[h] = mixed_blocks[128 * h : 128 * h + 128, WIDTH * h : WIDTH * h + WIDTH]
+
+    with jax.named_scope("feat"):
         for r in range(0, rows, chunk):
             here = pl.ds(r, chunk)
-            by_both = dot(sw_s[here, :], both, 1, 1)
-            dmf_s[here, WIDTH:] = by_both[:, WIDTH:].astype(BF16)
-            s_high, s_low = split(by_both[:, :WIDTH])
-            ds_s[here, :WIDTH] = s_high
-            ds_s[here, WIDTH:] = s_low
-        by_normed = dot(normed_s[...], dmf_s[:, WIDTH:], 0, 0)
-        by_slices = dot(ds_s[...], out_grad[...], 0, 0)
-        out_w = by_slices[:WIDTH] + by_slices[WIDTH:]
-        for h in range(NC):
-            half = slice(128 * h, 128 * h + 128)
-            for a, grad in enumerate((by_normed, out_w)):
-                for l in range(2):
-                    first = 8 * a + 4 * l
-                    pa[h, first : first + 4] = grad[half, 128 * l : 128 * l + 128].reshape(
-                        4, LOW, 8, 128
-                    )
+            dmf_s[here, WIDTH:] = dot(sw_s[here, :], totals_blocks, 1, 1).astype(BF16)
+        pack(pa, dot(normed_s[...], dmf_s[:, WIDTH:], 0, 0))
         swap(4, pa.at[1 - c], ra0)
+
+    with jax.named_scope("out"):
+        wait(15, rp2.at[pl.ds(0, NZ - 1)])
+        row_high, row_low = split(jnp.broadcast_to(jnp.sum(rp2[...], axis=0), (16, WIDTH)))
+        own = dot(row_high, mb_s[c], 1, 1) + dot(row_low, mb_s[c], 1, 1)
+        rp3[z] = own[:1] / everyone
+        send_all(16, column, NZ - 1, lambda i: rp3.at[z], rp3.at[z])
 
     w_both = jnp.concatenate([w_mid[...], w_feat[...]], axis=1)
 
@@ -454,26 +513,22 @@
         small += [slice_sum[d : d + 1] for d in range(DIM)]
         small += [jnp.zeros((1, 128), F32)] * (3 * NXY - len(small))
         small = jnp.concatenate(small, axis=0)
+        pack(pb, grad_mid)
         for h in range(NC):
-            for l in range(2):
-                pb[h, 8 * l : 8 * l + 8, 0:16, :] = grad_mid[
-                    128 * h : 128 * h + 128, 128 * l : 128 * l + 128
-                ].reshape(8, 16, 128)
             for k in range(NXY):
                 pb[h, k, 16:19, :] = small[3 * k : 3 * k + 3]
 
     with jax.named_scope("sumb_core"):
         swap(9, pb.at[1 - c], rb0)
-    with jax.named_scope("suma_plane"):
-        wait(5, ra1.at[pl.ds(0, NXY - 1)])
-        ra2[...] = jnp.sum(ra1[...], axis=0)
-        send_all(6, column_low, LOW - 1, lambda i: ra2.at[low_index(i)], ra3.at[zl])
-        ra3[zl] = ra2[zl]
     with jax.named_scope("sumb_plane"):
         wait(9, rb0)
         ab[...] = pb[c] + rb0[...]
         send_all(10, plane, NXY - 1, lambda i: ab.at[plane_index(i)], rb1.at[xy])
         rb1[xy] = ab[xy]
+    with jax.named_scope("suma_plane"):
+        wait(5, ra1.at[pl.ds(0, NXY - 1)])
+        ra2[zl] = jnp.sum(ra1[...], axis=0)
+        send_all(6, column_low, LOW - 1, lambda i: ra2.at[zl], ra2.at[zl])
 
     with jax.named_scope("points"):
         for r in range(0, rows, chunk):
@@ -486,35 +541,40 @@
         write(0)
 
     with jax.named_scope("suma_low"):
-        wait(6, ra3.at[pl.ds(0, LOW - 1)])
-        ra4[zh] = jnp.sum(ra3[...], axis=0)
-        send_all(7, column_high, NZH - 1, lambda i: ra4.at[zh], ra4.at[zh])
+        wait(6, ra2.at[pl.ds(0, LOW - 1)])
+        ra3[zh] = jnp.sum(ra2[...], axis=0)
+        send_all(7, column_high, NZH - 1, lambda i: ra3.at[zh], ra3.at[zh])
     with jax.named_scope("sumb_column"):
         wait(10, rb1.at[pl.ds(0, NXY - 1)])
         rb2[z] = jnp.sum(rb1[...], axis=0)
         send_all(11, column, NZ - 1, lambda i: rb2.at[z], rb2.at[z])
+    with jax.named_scope("out_column"):
+        wait(16, rp3.at[pl.ds(0, NZ - 1)])
+        rp4[xy] = jnp.concatenate([rp3[k] for k in range(NZ)], axis=0)
+        send_all(17, plane, NXY - 1, lambda i: rp4.at[xy], rp4.at[xy])
+    with jax.named_scope("token_grads"):
+        for n, out, back in zip((7, 8, 9), (o_q, o_k, o_v), backs):
+            out[...] = dot(tokens, back, 1, 1, HI) / everyone
+            write(n)
     with jax.named_scope("suma_high"):
-        wait(7, ra4.at[pl.ds(0, NZH - 1)])
-        ra5[xy, zl] = jnp.sum(ra4[...], axis=0) / everyone
-        send_all(8, column_low, LOW - 1, lambda i: ra5.at[xy, zl], ra5.at[xy, zl])
-        wait(8, ra5.at[xy, pl.ds(0, LOW - 1)])
-        send_all(12, plane, NXY - 1, lambda i: ra5.at[xy], ra5.at[xy])
+        wait(7, ra3.at[pl.ds(0, NZH - 1)])
+        ra4[xy] = jnp.sum(ra3[...], axis=0) / everyone
+        send_all(8, plane, NXY - 1, lambda i: ra4.at[xy], ra4.at[xy])
+    with jax.named_scope("out_last"):
+        wait(17, rp4.at[pl.ds(0, NXY - 1)])
+        o_out[...] = rp4[...].reshape(WIDTH, 128).T
+        write(10)
     with jax.named_scope("sumb_back"):
         wait(11, rb2.at[pl.ds(0, NZ - 1)])
         rb3[xy] = jnp.sum(rb2[...], axis=0) / everyone
-        send_all(13, plane, NXY - 1, lambda i: rb3.at[xy], rb3.at[xy])
+        send_all(12, plane, NXY - 1, lambda i: rb3.at[xy], rb3.at[xy])
     with jax.named_scope("suma_last"):
-        wait(12, ra5.at[pl.ds(0, NXY - 1)])
-        for a, out in enumerate((o_feat, o_out)):
-            for l in range(2):
-                first = 8 * a + 4 * l
-                out[:, 128 * l : 128 * l + 128] = ra5[first : first + 4].reshape(128, 128)
+        wait(8, ra4.at[pl.ds(0, NXY - 1)])
+        unpack(ra4, o_feat)
         write(4)
-        write(10)
     with jax.named_scope("sumb_last"):
-        wait(13, rb3.at[pl.ds(0, NXY - 1)])
-        for l in range(2):
-            o_mid[:, 128 * l : 128 * l + 128] = rb3[8 * l : 8 * l + 8, 0:16, :].reshape(128, 128)
+        wait(12, rb3.at[pl.ds(0, NXY - 1)])
+        unpack(rb3, o_mid)
         small = [rb3[k // 3, 16 + k % 3 : 17 + k % 3, :] for k in range(SMALL)]
         for l in range(2):
             o_gain[:, 128 * l : 128 * l + 128] = small[l]
@@ -612,7 +672,6 @@
             pltpu.VMEM((rows, COLS), BF16),
             pltpu.VMEM((rows, COLS), BF16),
             pltpu.VMEM((rows, 2 * WIDTH), BF16),
-            pltpu.VMEM((rows, 2 * WIDTH), BF16),
             pltpu.VMEM((rows, WIDTH), F32),
         ]
         + [
@@ -620,23 +679,25 @@
             for lead in ((NC, NXY), (NXY,), (NXY,), (NXY,), (NZ,), (NC * NXY,))
         ]
         + [
-            pltpu.VMEM(lead + (8, 128), F32)
-            for lead in (
-                (NC, NXY, LOW),
-                (NXY, LOW),
-                (NXY, LOW),
-                (NXY, LOW),
-                (LOW,),
-                (LOW,),
-                (NZH,),
-                (NXY, LOW),
-            )
+            pltpu.VMEM(lead + (16, 128), F32)
+            for lead in ((NC, NXY), (NXY,), (NXY,), (NXY,), (LOW,), (NZH,), (NXY,))
         ]
         + [
             pltpu.VMEM(lead + (ROWS2, 128), F32)
             for lead in ((NC, NXY), (NXY,), (NXY,), (NXY,), (NZ,), (NXY,))
         ]
-        + [pltpu.SemaphoreType.DMA((14,)), pltpu.SemaphoreType.DMA((14,))],
+        + [
+            pltpu.VMEM((NC, NXY, 16, WIDTH), F32),
+            pltpu.VMEM((NXY, 16, WIDTH), F32),
+            pltpu.VMEM((NXY, 16, WIDTH), F32),
+            pltpu.VMEM((NXY, 16, WIDTH), F32),
+            pltpu.VMEM((NZ, 1, WIDTH), F32),
+            pltpu.VMEM((NZ, 1, WIDTH), F32),
+            pltpu.VMEM((NZ, 1, 128), F32),
+            pltpu.VMEM((NXY, 16, 128), F32),
+            pltpu.VMEM((NC, 128, WIDTH), BF16),
+        ]
+        + [pltpu.SemaphoreType.DMA((18,)), pltpu.SemaphoreType.DMA((18,))],
         compiler_params=pltpu.CompilerParams(
             collective_id=0, has_side_effects=True, vmem_limit_bytes=VMEM_BYTES
         ),

time: 74.3 us -> 69.7 us (0.938)
  the two profiles are of different devices: /device:TPU:2 before, /device:TPU:1 now
where the time goes in v3:
time: 69.7 us; the launch traced here: 69.6 us
  Pallas kernels  68.9 us (99%)
    pallas_call x1, Pallas kernels, shards(): pl.pallas_call(functools.partial(kernel, float(everyone), 128), out_shape...  66.9 us
    pallas_call x1, Pallas kernels, shards(): pl.pallas_call(functools.partial(hand_on, len(outs)), out_shape=out_shape...  2.02 us

profile of v3, /device:TPU:1, one launch (start us, length us, event | category | flops | bytes accessed | tf_op | source)
XLA Modules:
  0.0 69.6 jit_solution(14260464982531993476)
XLA Ops:
  0.6 66.9 %backward.1 = (bf16[512,256]{1,0:T(8,128)(2,1)}, f32[1,256]{1,0:T(1,128)}, f32[1,256]{1,0:T(1,128)}, f32[128,256]{1,0:T(8,128)}, f32[128,256]{1,0:T(8,128)}, /*i...) custom-call(bf16[512,256]{1,0:T(8,128)(2,1)} %points_h.1, ...), custom_call_target="tpu_custom_call" | custom-call | tf_op jit(solution)/shard_map/backward/pallas_call | solution.py:654
  67.5 2.0 %hand_on.1 = (bf16[512,256]{1,0:T(8,128)(2,1)}, f32[1,256]{1,0:T(1,128)}, f32[1,256]{1,0:T(1,128)}, f32[128,256]{1,0:T(8,128)}, f32[128,256]{1,0:T(8,128)}, /*in...) custom-call(bf16[512,256]{1,0:T(8,128)(2,1)} %get-tuple-element.33.r, ...), custom_call_target="tpu_custom_call" | custom-call | tf_op jit(solution)/shard_map/hand_on/pallas_call | solution.py:706

commit v4 on v3

--- a/solution.py
+++ b/solution.py
@@ -18,9 +18,9 @@
 NXY = NX * NY
 LOW = 4
 NZH = NZ // LOW
-ROWS1, ROWS2 = 9, 19
+ROWS1, ROWS2, ROWS3 = 9, 16, 3
 SMALL = 40
-VMEM_BYTES = 60 * 1024 * 1024
+VMEM_BYTES = 48 * 1024 * 1024
 BF_MAX = 3.3895314e38
 
 
@@ -144,17 +144,6 @@
     wk_h,
     wv_h,
     w_out_h,
-    h_points,
-    h_gain,
-    h_bias,
-    h_mid,
-    h_feat,
-    h_slice,
-    h_temper,
-    h_q,
-    h_k,
-    h_v,
-    h_out,
     o_points,
     o_gain,
     o_bias,
@@ -166,7 +155,6 @@
     o_k,
     o_v,
     o_out,
-    stores,
     points,
     out_grad,
     gain_ref,
@@ -193,8 +181,6 @@
     dmf_s,
     dn_s,
     p1,
-    r10,
-    a1,
     r11,
     r12,
     r13,
@@ -220,6 +206,12 @@
     rp3,
     rp4,
     mb_s,
+    ps,
+    rs0,
+    as_,
+    rs1,
+    rs2,
+    rs3,
     sends,
     recvs,
 ):
@@ -272,21 +264,6 @@
         return (xy * NZ + (z + LOW * far_first(i)) % NZ, c)
 
     sibling = (p, 1 - c)
-    made = (
-        (o_points, h_points),
-        (o_gain, h_gain),
-        (o_bias, h_bias),
-        (o_mid, h_mid),
-        (o_feat, h_feat),
-        (o_slice, h_slice),
-        (o_temper, h_temper),
-        (o_q, h_q),
-        (o_k, h_k),
-        (o_v, h_v),
-        (o_out, h_out),
-    )
-    writes = [pltpu.make_async_copy(a, b, stores.at[n]) for n, (a, b) in enumerate(made)]
-
     barrier = pltpu.get_barrier_semaphore()
 
     greetings = [(plane_cores, i) for i in range(2 * NXY - 1)]
@@ -298,7 +275,10 @@
             pl.semaphore_signal(barrier, inc=1, device_id=who(i), device_id_type=MESH)
         del greetings[:count]
 
-    unsent, started = [], []
+    with jax.named_scope("greet"):
+        greet(n_greetings)
+
+    unsent = []
 
     def pack(ref, grad):
         for h in range(NC):
@@ -329,10 +309,6 @@
         )
         copy.wait_recv()
         unsent.append(copy)
-
-    def write(n):
-        writes[n].start()
-        started.append(writes[n])
 
     ones = (iota((256, 256), 0) // SLICES == iota((256, 256), 1) // SLICES).astype(F32).astype(BF16)
 
@@ -351,7 +327,6 @@
     with jax.named_scope("front"):
         for r in range(0, rows, chunk):
             here = pl.ds(r, chunk)
-            greet(-(-n_greetings * chunk // rows))
             xs = points[here, :].astype(F32)
             center = xs - jnp.mean(xs, axis=1, keepdims=True)
             rstd = lax.rsqrt(jnp.mean(center * center, axis=1, keepdims=True) + 1e-05)
@@ -398,22 +373,25 @@
     with jax.named_scope("barrier"):
         pl.semaphore_wait(barrier, n_greetings)
 
-    with jax.named_scope("sum1_core"):
-        swap(0, p1.at[1 - c], r10)
-        token_weights = (wq[...], wk[...], wv[...])
-        forward_terms = jnp.concatenate([weight_terms(w.T) for w in token_weights], axis=0)
-        backward_terms = jnp.concatenate([weight_terms(w) for w in token_weights], axis=1)
+    me1 = c * NXY + xy
+    with jax.named_scope("sum1_plane"):
+        send_all(
+            1,
+            plane_cores,
+            2 * NXY - 1,
+            lambda i: p1.at[(c + 1 + i % 2) % NC, plane_index(i // 2)],
+            r11.at[me1],
+        )
+        r11[me1] = p1[c, xy]
         projected = dot(out_grad[...], sw, 0, 0)
         for h in range(NC):
             half = projected[:, WIDTH * h : WIDTH * h + WIDTH]
             pp[h] = half.reshape(NXY, 16, WIDTH)
-        wait(0, r10)
-        a1[...] = p1[c] + r10[...]
-    with jax.named_scope("sum1_plane"):
-        send_all(1, plane, NXY - 1, lambda i: a1.at[plane_index(i)], r11.at[xy])
         swap(13, pp.at[1 - c], rp0)
-        r11[xy] = a1[xy]
-        wait(1, r11.at[pl.ds(0, NXY - 1)])
+        token_weights = (wq[...], wk[...], wv[...])
+        forward_terms = jnp.concatenate([weight_terms(w.T) for w in token_weights], axis=0)
+        backward_terms = jnp.concatenate([weight_terms(w) for w in token_weights], axis=1)
+        wait(1, r11.at[pl.ds(0, 2 * NXY - 1)])
         r12[z] = jnp.sum(r11[...], axis=0)
     with jax.named_scope("sum1_column"):
         send_all(2, column, NZ - 1, lambda i: r12.at[z], r12.at[z])
@@ -422,7 +400,6 @@
         send_all(14, plane, NXY - 1, lambda i: ap.at[plane_index(i)], rp1.at[xy])
         rp1[xy] = ap[xy]
         wait(2, r12.at[pl.ds(0, NZ - 1)])
-        me1 = c * NXY + xy
         r13[me1] = jnp.sum(r12[...], axis=0)
     with jax.named_scope("sum1_back"):
         send_all(3, plane_cores, 2 * NXY - 1, lambda i: r13.at[me1], r13.at[me1])
@@ -487,6 +464,9 @@
         sc_s[here, :] = scaled
         sums[0] += fold(d_logits * logits_s[here, :])
         dmf_s[here, :WIDTH] = dot(scaled, slice_blocks, 1, 1).astype(BF16)
+
+    def norm(r):
+        here = pl.ds(r, chunk)
         d_normed = dot(dmf_s[here, :], w_both, 1, 1)
         dn_s[here, :] = d_normed
         sums[1] += fold(d_normed * xhat_s[here, :])
@@ -503,23 +483,23 @@
     with jax.named_scope("back_second"):
         for r in range(rows // 2, rows, chunk):
             back(r)
-    with jax.named_scope("sharesb"):
-        grad_mid = dot(normed_s[...], dmf_s[:, :WIDTH], 0, 0)
+    with jax.named_scope("sumb_core"):
+        pack(pb, dot(normed_s[...], dmf_s[:, :WIDTH], 0, 0))
+        swap(9, pb.at[1 - c], rb0)
+    with jax.named_scope("shares_small"):
+        for r in range(0, rows, chunk):
+            norm(r)
         slice_sum = sum(diagonal_rows(dot(mid_s[...], sc_s[...], 0, 0)))
         temper_sum, gain_sum, bias_sum = (jnp.sum(v, axis=0, keepdims=True) for v in sums)
         small = [gain_sum[:, 128 * l : 128 * l + 128] for l in range(2)]
         small += [bias_sum[:, 128 * l : 128 * l + 128] for l in range(2)]
         small += [temper_sum[:, 128 * l : 128 * l + 128] for l in range(4)]
-        small += [slice_sum[d : d + 1] for d in range(DIM)]
-        small += [jnp.zeros((1, 128), F32)] * (3 * NXY - len(small))
+        small += [slice_sum, jnp.zeros((ROWS3 * NXY - SMALL, 128), F32)]
         small = jnp.concatenate(small, axis=0)
-        pack(pb, grad_mid)
-        for h in range(NC):
-            for k in range(NXY):
-                pb[h, k, 16:19, :] = small[3 * k : 3 * k + 3]
-
-    with jax.named_scope("sumb_core"):
-        swap(9, pb.at[1 - c], rb0)
+        for k in range(NXY):
+            ps[k] = small[ROWS3 * k : ROWS3 * k + ROWS3]
+        swap(0, ps, rs0)
+
     with jax.named_scope("sumb_plane"):
         wait(9, rb0)
         ab[...] = pb[c] + rb0[...]
@@ -530,6 +510,11 @@
         ra2[zl] = jnp.sum(ra1[...], axis=0)
         send_all(6, column_low, LOW - 1, lambda i: ra2.at[zl], ra2.at[zl])
 
+    with jax.named_scope("small_plane"):
+        wait(0, rs0)
+        as_[...] = ps[...] + rs0[...]
+        send_all(18, plane, NXY - 1, lambda i: as_.at[plane_index(i)], rs1.at[xy])
+        rs1[xy] = as_[xy]
     with jax.named_scope("points"):
         for r in range(0, rows, chunk):
             here = pl.ds(r, chunk)
@@ -538,7 +523,6 @@
             inner = d_xhat - jnp.mean(d_xhat, axis=1, keepdims=True)
             inner = inner - xhat * jnp.mean(d_xhat * xhat, axis=1, keepdims=True)
             o_points[here, :] = (inner * rstd_s[here, 0:1]).astype(BF16)
-        write(0)
 
     with jax.named_scope("suma_low"):
         wait(6, ra2.at[pl.ds(0, LOW - 1)])
@@ -552,10 +536,13 @@
         wait(16, rp3.at[pl.ds(0, NZ - 1)])
         rp4[xy] = jnp.concatenate([rp3[k] for k in range(NZ)], axis=0)
         send_all(17, plane, NXY - 1, lambda i: rp4.at[xy], rp4.at[xy])
+    with jax.named_scope("small_column"):
+        wait(18, rs1.at[pl.ds(0, NXY - 1)])
+        rs2[z] = jnp.sum(rs1[...], axis=0)
+        send_all(19, column, NZ - 1, lambda i: rs2.at[z], rs2.at[z])
     with jax.named_scope("token_grads"):
-        for n, out, back in zip((7, 8, 9), (o_q, o_k, o_v), backs):
-            out[...] = dot(tokens, back, 1, 1, HI) / everyone
-            write(n)
+        for out, grad in zip((o_q, o_k, o_v), backs):
+            out[...] = dot(tokens, grad, 1, 1, HI) / everyone
     with jax.named_scope("suma_high"):
         wait(7, ra3.at[pl.ds(0, NZH - 1)])
         ra4[xy] = jnp.sum(ra3[...], axis=0) / everyone
@@ -563,19 +550,20 @@
     with jax.named_scope("out_last"):
         wait(17, rp4.at[pl.ds(0, NXY - 1)])
         o_out[...] = rp4[...].reshape(WIDTH, 128).T
-        write(10)
     with jax.named_scope("sumb_back"):
         wait(11, rb2.at[pl.ds(0, NZ - 1)])
         rb3[xy] = jnp.sum(rb2[...], axis=0) / everyone
         send_all(12, plane, NXY - 1, lambda i: rb3.at[xy], rb3.at[xy])
+    with jax.named_scope("small_back"):
+        wait(19, rs2.at[pl.ds(0, NZ - 1)])
+        rs3[xy] = jnp.sum(rs2[...], axis=0) / everyone
+        send_all(20, plane, NXY - 1, lambda i: rs3.at[xy], rs3.at[xy])
     with jax.named_scope("suma_last"):
         wait(8, ra4.at[pl.ds(0, NXY - 1)])
         unpack(ra4, o_feat)
-        write(4)
-    with jax.named_scope("sumb_last"):
-        wait(12, rb3.at[pl.ds(0, NXY - 1)])
-        unpack(rb3, o_mid)
-        small = [rb3[k // 3, 16 + k % 3 : 17 + k % 3, :] for k in range(SMALL)]
+    with jax.named_scope("small_last"):
+        wait(20, rs3.at[pl.ds(0, NXY - 1)])
+        small = [rs3[k // ROWS3, k % ROWS3 : k % ROWS3 + 1, :] for k in range(SMALL)]
         for l in range(2):
             o_gain[:, 128 * l : 128 * l + 128] = small[l]
             o_bias[:, 128 * l : 128 * l + 128] = small[2 + l]
@@ -589,31 +577,21 @@
                 part = jnp.sum(part, axis=1, keepdims=True)
                 d_temper = jnp.where(place == 2 * g + s, part, d_temper)
         o_temper[...] = -d_temper / temper[...]
-        for n in (1, 2, 3, 5, 6):
-            write(n)
+    with jax.named_scope("sumb_last"):
+        wait(12, rb3.at[pl.ds(0, NXY - 1)])
+        unpack(rb3, o_mid)
 
     with jax.named_scope("done"):
         for copy in unsent:
             copy.wait_send()
-        for copy in started:
-            copy.wait()
 
 
 def hand_on(count, *refs):
-    ins, outs, held, (loads, stores) = (
-        refs[:count],
-        refs[count : 2 * count],
-        refs[2 * count : 3 * count],
-        refs[3 * count :],
-    )
-    one = [pltpu.make_async_copy(ins[n], held[n], loads.at[n]) for n in range(count)]
-    two = [pltpu.make_async_copy(held[n], outs[n], stores.at[n]) for n in range(count)]
-    for copy in one:
+    sems = refs[2 * count]
+    copies = [pltpu.make_async_copy(refs[n], refs[count + n], sems.at[n]) for n in range(count)]
+    for copy in copies:
         copy.start()
-    for first, second in zip(one, two):
-        first.wait()
-        second.start()
-    for copy in two:
+    for copy in copies:
         copy.wait()
 
 
@@ -623,6 +601,7 @@
     rows = points.shape[0]
     everyone = rows * NXY * NZ * NC
     hbm = pl.BlockSpec(memory_space=pltpu.HBM)
+    vmem = pl.BlockSpec(memory_space=pltpu.VMEM)
     f = lambda *s: jax.ShapeDtypeStruct(s, F32)
     args = (
         points,
@@ -655,10 +634,8 @@
         functools.partial(kernel, float(everyone), 128),
         out_shape=out_shape,
         in_specs=[hbm] * 12,
-        out_specs=(hbm,) * 11,
-        scratch_shapes=[pltpu.VMEM(a.shape, a.dtype) for a in out_shape]
-        + [pltpu.SemaphoreType.DMA((11,))]
-        + [pltpu.VMEM(a.shape, a.dtype) for a in args]
+        out_specs=(vmem,) * 11,
+        scratch_shapes=[pltpu.VMEM(a.shape, a.dtype) for a in args]
         + [pltpu.SemaphoreType.DMA((12,))]
         + [
             pltpu.VMEM((rows, WIDTH), F32),
@@ -676,7 +653,7 @@
         ]
         + [
             pltpu.VMEM(lead + (ROWS1, 128), F32)
-            for lead in ((NC, NXY), (NXY,), (NXY,), (NXY,), (NZ,), (NC * NXY,))
+            for lead in ((NC, NXY), (NC * NXY,), (NZ,), (NC * NXY,))
         ]
         + [
             pltpu.VMEM(lead + (16, 128), F32)
@@ -697,22 +674,24 @@
             pltpu.VMEM((NXY, 16, 128), F32),
             pltpu.VMEM((NC, 128, WIDTH), BF16),
         ]
-        + [pltpu.SemaphoreType.DMA((18,)), pltpu.SemaphoreType.DMA((18,))],
+        + [
+            pltpu.VMEM((lead, ROWS3, 128), F32)
+            for lead in (NXY, NXY, NXY, NXY, NZ, NXY)
+        ]
+        + [pltpu.SemaphoreType.DMA((21,)), pltpu.SemaphoreType.DMA((21,))],
         compiler_params=pltpu.CompilerParams(
             collective_id=0, has_side_effects=True, vmem_limit_bytes=VMEM_BYTES
         ),
         name="backward",
-    )(*args)
+    )(*[pltpu.with_memory_space_constraint(a, pltpu.HBM) for a in args])
     outs = pl.pallas_call(
         functools.partial(hand_on, len(outs)),
         out_shape=out_shape,
-        in_specs=[hbm] * 11,
+        in_specs=[vmem] * 11,
         out_specs=(hbm,) * 11,
-        scratch_shapes=[pltpu.VMEM(a.shape, a.dtype) for a in out_shape]
-        + [pltpu.SemaphoreType.DMA((11,))] * 2,
-        compiler_params=pltpu.CompilerParams(vmem_limit_bytes=VMEM_BYTES),
+        scratch_shapes=[pltpu.SemaphoreType.DMA((11,))],
         name="hand_on",
-    )(*outs)
+    )(*[pltpu.with_memory_space_constraint(o, pltpu.VMEM) for o in outs])
     outs = list(outs)
     for n in (1, 2, 6):
         outs[n] = outs[n].reshape(-1)

time: 69.7 us -> 65.8 us (0.944)
  Pallas kernels: 68.9 us -> 64.5 us
    pallas_call x1, Pallas kernels: 66.9 us -> 63.5 us  [shards(): pl.pallas_call(functools.partial(kernel, float(everyone), 128), out_shape...]
    pallas_call x1, Pallas kernels: 2.02 us -> 0.97 us  [shards(): pl.pallas_call(functools.partial(hand_on, len(outs)), out_shape=out_shape...]
where the time goes in v4:
time: 65.8 us; the launch traced here: 65.1 us
  Pallas kernels  64.5 us (98%)
  between operations  0.66 us (1%)
    pallas_call x1, Pallas kernels, shards(): pl.pallas_call(functools.partial(kernel, float(everyone), 128), out_shape...  63.5 us

profile of v4, /device:TPU:1, one launch (start us, length us, event | category | flops | bytes accessed | tf_op | source)
XLA Modules:
  0.0 65.1 jit_solution(6462222589077410908)
XLA Ops:
  0.6 63.5 %backward.1 = (bf16[512,256]{1,0:T(8,128)(2,1)S(1)}, f32[1,256]{1,0:T(1,128)S(1)}, f32[1,256]{1,0:T(1,128)S(1)}, f32[128,256]{1,0:T(8,128)S(1)}, f32[128,256]{1,...) custom-call(bf16[512,256]{1,0:T(8,128)(2,1)} %points_h.1, ...), custom_call_target="tpu_custom_call" | custom-call | tf_op jit(solution)/shard_map/backward/pallas_call | solution.py:633
  64.2 1.0 %hand_on.1 = (bf16[512,256]{1,0:T(8,128)(2,1)}, f32[1,256]{1,0:T(1,128)}, f32[1,256]{1,0:T(1,128)}, f32[128,256]{1,0:T(8,128)}, f32[128,256]{1,0:T(8,128)}, /*in...) custom-call(bf16[512,256]{1,0:T(8,128)(2,1)S(1)} %get-tuple-element., ...), custom_call_target="tpu_custom_call" | custom-call | tf_op jit(solution)/shard_map/hand_on/pallas_call | solution.py:687

commit v5 on v4

--- a/solution.py
+++ b/solution.py
@@ -16,8 +16,6 @@
 COLS = HEADS * SLICES
 NX, NY, NZ, NC = 4, 4, 16, 2
 NXY = NX * NY
-LOW = 4
-NZH = NZ // LOW
 ROWS1, ROWS2, ROWS3 = 9, 16, 3
 SMALL = 40
 VMEM_BYTES = 48 * 1024 * 1024
@@ -184,13 +182,6 @@
     r11,
     r12,
     r13,
-    pa,
-    ra0,
-    aa,
-    ra1,
-    ra2,
-    ra3,
-    ra4,
     pb,
     rb0,
     ab,
@@ -206,6 +197,7 @@
     rp3,
     rp4,
     mb_s,
+    tb_s,
     ps,
     rs0,
     as_,
@@ -236,7 +228,6 @@
     p, c = lax.axis_index("pts"), lax.axis_index("rep")
     x, y, z = p // (NY * NZ), p // NZ % NY, p % NZ
     xy = x * NY + y
-    zl, zh = z % LOW, z // LOW
     rows = points.shape[0]
 
     def plane_index(i):
@@ -253,15 +244,6 @@
 
     def column(i):
         return (xy * NZ + column_index(i), c)
-
-    def low_index(i):
-        return (zl + far_first(i)) % LOW
-
-    def column_low(i):
-        return (xy * NZ + zh * LOW + low_index(i), c)
-
-    def column_high(i):
-        return (xy * NZ + (z + LOW * far_first(i)) % NZ, c)
 
     sibling = (p, 1 - c)
     barrier = pltpu.get_barrier_semaphore()
@@ -384,9 +366,13 @@
         )
         r11[me1] = p1[c, xy]
         projected = dot(out_grad[...], sw, 0, 0)
+        by_normed = dot(normed_s[...], sw, 0, 0)
         for h in range(NC):
             half = projected[:, WIDTH * h : WIDTH * h + WIDTH]
-            pp[h] = half.reshape(NXY, 16, WIDTH)
+            pp[h, :, 0:16, :] = half.reshape(NXY, 16, WIDTH)
+            for l in range(2):
+                half = by_normed[128 * h : 128 * h + 128, WIDTH * l : WIDTH * l + WIDTH]
+                pp[h, :, 16 + 8 * l : 24 + 8 * l, :] = half.reshape(NXY, 8, WIDTH)
         swap(13, pp.at[1 - c], rp0)
         token_weights = (wq[...], wk[...], wv[...])
         forward_terms = jnp.concatenate([weight_terms(w.T) for w in token_weights], axis=0)
@@ -406,7 +392,8 @@
         wait(14, rp1.at[pl.ds(0, NXY - 1)])
         piece = jnp.sum(rp1[...], axis=0)
         for k in range(NZ):
-            sp[k] = piece[k : k + 1]
+            sp[k, 0:1] = piece[k : k + 1]
+            sp[k, 1:2] = piece[16 + k : 17 + k]
         send_all(15, column, NZ - 1, lambda i: sp.at[column_index(i)], rp2.at[z])
         rp2[z] = sp[z]
         wait(3, r13.at[pl.ds(0, 2 * NXY - 1)])
@@ -431,21 +418,9 @@
         totals_blocks = block_diagonal(d_totals.astype(BF16).astype(F32)).astype(BF16)
         both = jnp.concatenate([mixed_blocks, totals_blocks], axis=0)
         for h in range(NC):
-            mb_s[h] = mixed_blocks[128 * h : 128 * h + 128, WIDTH * h : WIDTH * h + WIDTH]
-
-    with jax.named_scope("feat"):
-        for r in range(0, rows, chunk):
-            here = pl.ds(r, chunk)
-            dmf_s[here, WIDTH:] = dot(sw_s[here, :], totals_blocks, 1, 1).astype(BF16)
-        pack(pa, dot(normed_s[...], dmf_s[:, WIDTH:], 0, 0))
-        swap(4, pa.at[1 - c], ra0)
-
-    with jax.named_scope("out"):
-        wait(15, rp2.at[pl.ds(0, NZ - 1)])
-        row_high, row_low = split(jnp.broadcast_to(jnp.sum(rp2[...], axis=0), (16, WIDTH)))
-        own = dot(row_high, mb_s[c], 1, 1) + dot(row_low, mb_s[c], 1, 1)
-        rp3[z] = own[:1] / everyone
-        send_all(16, column, NZ - 1, lambda i: rp3.at[z], rp3.at[z])
+            part = (slice(128 * h, 128 * h + 128), slice(WIDTH * h, WIDTH * h + WIDTH))
+            mb_s[h] = mixed_blocks[part]
+            tb_s[h] = totals_blocks[part]
 
     w_both = jnp.concatenate([w_mid[...], w_feat[...]], axis=1)
 
@@ -467,27 +442,27 @@
 
     def norm(r):
         here = pl.ds(r, chunk)
+        dmf_s[here, WIDTH:] = dot(sw_s[here, :], totals_blocks, 1, 1).astype(BF16)
         d_normed = dot(dmf_s[here, :], w_both, 1, 1)
         dn_s[here, :] = d_normed
         sums[1] += fold(d_normed * xhat_s[here, :])
         sums[2] += fold(d_normed)
 
-    with jax.named_scope("back_first"):
-        for r in range(0, rows // 2, chunk):
-            back(r)
-    with jax.named_scope("suma_core"):
-        wait(4, ra0)
-        aa[...] = pa[c] + ra0[...]
-        send_all(5, plane, NXY - 1, lambda i: aa.at[plane_index(i)], ra1.at[xy])
-        ra1[xy] = aa[xy]
-    with jax.named_scope("back_second"):
-        for r in range(rows // 2, rows, chunk):
+    with jax.named_scope("back"):
+        for r in range(0, rows, chunk):
             back(r)
     with jax.named_scope("sumb_core"):
         pack(pb, dot(normed_s[...], dmf_s[:, :WIDTH], 0, 0))
         swap(9, pb.at[1 - c], rb0)
+        for r in range(0, rows // 2, chunk):
+            norm(r)
+    with jax.named_scope("sumb_plane"):
+        wait(9, rb0)
+        ab[...] = pb[c] + rb0[...]
+        send_all(10, plane, NXY - 1, lambda i: ab.at[plane_index(i)], rb1.at[xy])
+        rb1[xy] = ab[xy]
     with jax.named_scope("shares_small"):
-        for r in range(0, rows, chunk):
+        for r in range(rows // 2, rows, chunk):
             norm(r)
         slice_sum = sum(diagonal_rows(dot(mid_s[...], sc_s[...], 0, 0)))
         temper_sum, gain_sum, bias_sum = (jnp.sum(v, axis=0, keepdims=True) for v in sums)
@@ -500,15 +475,14 @@
             ps[k] = small[ROWS3 * k : ROWS3 * k + ROWS3]
         swap(0, ps, rs0)
 
-    with jax.named_scope("sumb_plane"):
-        wait(9, rb0)
-        ab[...] = pb[c] + rb0[...]
-        send_all(10, plane, NXY - 1, lambda i: ab.at[plane_index(i)], rb1.at[xy])
-        rb1[xy] = ab[xy]
-    with jax.named_scope("suma_plane"):
-        wait(5, ra1.at[pl.ds(0, NXY - 1)])
-        ra2[zl] = jnp.sum(ra1[...], axis=0)
-        send_all(6, column_low, LOW - 1, lambda i: ra2.at[zl], ra2.at[zl])
+    with jax.named_scope("out_feat"):
+        wait(15, rp2.at[pl.ds(0, NZ - 1)])
+        summed = jnp.sum(rp2[...], axis=0)
+        for n, blocks in enumerate((mb_s[c], tb_s[z // 8])):
+            row_high, row_low = split(jnp.broadcast_to(summed[n : n + 1], (16, WIDTH)))
+            own = dot(row_high, blocks, 1, 1) + dot(row_low, blocks, 1, 1)
+            rp3[z, n : n + 1] = own[:1] / everyone
+        send_all(16, column, NZ - 1, lambda i: rp3.at[z], rp3.at[z])
 
     with jax.named_scope("small_plane"):
         wait(0, rs0)
@@ -524,32 +498,27 @@
             inner = inner - xhat * jnp.mean(d_xhat * xhat, axis=1, keepdims=True)
             o_points[here, :] = (inner * rstd_s[here, 0:1]).astype(BF16)
 
-    with jax.named_scope("suma_low"):
-        wait(6, ra2.at[pl.ds(0, LOW - 1)])
-        ra3[zh] = jnp.sum(ra2[...], axis=0)
-        send_all(7, column_high, NZH - 1, lambda i: ra3.at[zh], ra3.at[zh])
     with jax.named_scope("sumb_column"):
         wait(10, rb1.at[pl.ds(0, NXY - 1)])
         rb2[z] = jnp.sum(rb1[...], axis=0)
         send_all(11, column, NZ - 1, lambda i: rb2.at[z], rb2.at[z])
-    with jax.named_scope("out_column"):
-        wait(16, rp3.at[pl.ds(0, NZ - 1)])
-        rp4[xy] = jnp.concatenate([rp3[k] for k in range(NZ)], axis=0)
-        send_all(17, plane, NXY - 1, lambda i: rp4.at[xy], rp4.at[xy])
     with jax.named_scope("small_column"):
         wait(18, rs1.at[pl.ds(0, NXY - 1)])
         rs2[z] = jnp.sum(rs1[...], axis=0)
         send_all(19, column, NZ - 1, lambda i: rs2.at[z], rs2.at[z])
+    with jax.named_scope("out_column"):
+        wait(16, rp3.at[pl.ds(0, NZ - 1)])
+        for n in range(2):
+            rp4[xy, n] = jnp.concatenate([rp3[k, n : n + 1] for k in range(NZ)], axis=0)
+        send_all(17, plane, NXY - 1, lambda i: rp4.at[xy], rp4.at[xy])
     with jax.named_scope("token_grads"):
         for out, grad in zip((o_q, o_k, o_v), backs):
             out[...] = dot(tokens, grad, 1, 1, HI) / everyone
-    with jax.named_scope("suma_high"):
-        wait(7, ra3.at[pl.ds(0, NZH - 1)])
-        ra4[xy] = jnp.sum(ra3[...], axis=0) / everyone
-        send_all(8, plane, NXY - 1, lambda i: ra4.at[xy], ra4.at[xy])
     with jax.named_scope("out_last"):
         wait(17, rp4.at[pl.ds(0, NXY - 1)])
-        o_out[...] = rp4[...].reshape(WIDTH, 128).T
+        o_out[...] = rp4[:, 0].reshape(WIDTH, 128).T
+        for l in range(2):
+            o_feat[:, 128 * l : 128 * l + 128] = rp4[:, 1, 8 * l : 8 * l + 8, :].reshape(128, 128)
     with jax.named_scope("sumb_back"):
         wait(11, rb2.at[pl.ds(0, NZ - 1)])
         rb3[xy] = jnp.sum(rb2[...], axis=0) / everyone
@@ -558,9 +527,6 @@
         wait(19, rs2.at[pl.ds(0, NZ - 1)])
         rs3[xy] = jnp.sum(rs2[...], axis=0) / everyone
         send_all(20, plane, NXY - 1, lambda i: rs3.at[xy], rs3.at[xy])
-    with jax.named_scope("suma_last"):
-        wait(8, ra4.at[pl.ds(0, NXY - 1)])
-        unpack(ra4, o_feat)
     with jax.named_scope("small_last"):
         wait(20, rs3.at[pl.ds(0, NXY - 1)])
         small = [rs3[k // ROWS3, k % ROWS3 : k % ROWS3 + 1, :] for k in range(SMALL)]
@@ -631,7 +597,7 @@
         f(128, WIDTH),
     )
     outs = pl.pallas_call(
-        functools.partial(kernel, float(everyone), 128),
+        functools.partial(kernel, float(everyone), 256),
         out_shape=out_shape,
         in_specs=[hbm] * 12,
         out_specs=(vmem,) * 11,
@@ -656,22 +622,19 @@
             for lead in ((NC, NXY), (NC * NXY,), (NZ,), (NC * NXY,))
         ]
         + [
-            pltpu.VMEM(lead + (16, 128), F32)
-            for lead in ((NC, NXY), (NXY,), (NXY,), (NXY,), (LOW,), (NZH,), (NXY,))
-        ]
-        + [
             pltpu.VMEM(lead + (ROWS2, 128), F32)
             for lead in ((NC, NXY), (NXY,), (NXY,), (NXY,), (NZ,), (NXY,))
         ]
         + [
-            pltpu.VMEM((NC, NXY, 16, WIDTH), F32),
-            pltpu.VMEM((NXY, 16, WIDTH), F32),
-            pltpu.VMEM((NXY, 16, WIDTH), F32),
-            pltpu.VMEM((NXY, 16, WIDTH), F32),
-            pltpu.VMEM((NZ, 1, WIDTH), F32),
-            pltpu.VMEM((NZ, 1, WIDTH), F32),
-            pltpu.VMEM((NZ, 1, 128), F32),
-            pltpu.VMEM((NXY, 16, 128), F32),
+            pltpu.VMEM((NC, NXY, 32, WIDTH), F32),
+            pltpu.VMEM((NXY, 32, WIDTH), F32),
+            pltpu.VMEM((NXY, 32, WIDTH), F32),
+            pltpu.VMEM((NXY, 32, WIDTH), F32),
+            pltpu.VMEM((NZ, 2, WIDTH), F32),
+            pltpu.VMEM((NZ, 2, WIDTH), F32),
+            pltpu.VMEM((NZ, 2, 128), F32),
+            pltpu.VMEM((NXY, 2, 16, 128), F32),
+            pltpu.VMEM((NC, 128, WIDTH), BF16),
             pltpu.VMEM((NC, 128, WIDTH), BF16),
         ]
         + [

time: 65.8 us -> 62.4 us (0.948)
  Pallas kernels: 64.5 us -> 60.9 us
    pallas_call x1, Pallas kernels: 63.5 us -> 60 us  [shards(): pl.pallas_call(functools.partial(kernel, float(everyone), 256), out_shape...]
where the time goes in v5:
time: 62.4 us; the launch traced here: 61.6 us
  Pallas kernels  60.9 us (98%)
  between operations  0.66 us (1%)
    pallas_call x1, Pallas kernels, shards(): pl.pallas_call(functools.partial(kernel, float(everyone), 256), out_shape...  60 us

profile of v5, /device:TPU:1, one launch (start us, length us, event | category | flops | bytes accessed | tf_op | source)
XLA Modules:
  0.0 61.6 jit_solution(4264438898519219147)
XLA Ops:
  0.6 60.0 %backward.1 = (bf16[512,256]{1,0:T(8,128)(2,1)S(1)}, f32[1,256]{1,0:T(1,128)S(1)}, f32[1,256]{1,0:T(1,128)S(1)}, f32[128,256]{1,0:T(8,128)S(1)}, f32[128,256]{1,...) custom-call(bf16[512,256]{1,0:T(8,128)(2,1)} %points_h.1, ...), custom_call_target="tpu_custom_call" | custom-call | tf_op jit(solution)/shard_map/backward/pallas_call | solution.py:599
  60.6 1.0 %hand_on.1 = (bf16[512,256]{1,0:T(8,128)(2,1)}, f32[1,256]{1,0:T(1,128)}, f32[1,256]{1,0:T(1,128)}, f32[128,256]{1,0:T(8,128)}, f32[128,256]{1,0:T(8,128)}, /*in...) custom-call(bf16[512,256]{1,0:T(8,128)(2,1)S(1)} %get-tuple-element., ...), custom_call_target="tpu_custom_call" | custom-call | tf_op jit(solution)/shard_map/hand_on/pallas_call | solution.py:650

commit v6 on v5

--- a/solution.py
+++ b/solution.py
@@ -280,7 +280,11 @@
             ).start()
             return 0
 
-        lax.fori_loop(0, count, body, 0)
+        if count < NXY:
+            for i in range(count):
+                body(i, 0)
+        else:
+            lax.fori_loop(0, count, body, 0)
 
     def swap(stage, src, dst):
         send_all(stage, lambda i: sibling, 1, lambda i: src, dst)
@@ -489,6 +493,10 @@
         as_[...] = ps[...] + rs0[...]
         send_all(18, plane, NXY - 1, lambda i: as_.at[plane_index(i)], rs1.at[xy])
         rs1[xy] = as_[xy]
+    with jax.named_scope("sumb_column"):
+        wait(10, rb1.at[pl.ds(0, NXY - 1)])
+        rb2[z] = jnp.sum(rb1[...], axis=0)
+        send_all(11, column, NZ - 1, lambda i: rb2.at[z], rb2.at[z])
     with jax.named_scope("points"):
         for r in range(0, rows, chunk):
             here = pl.ds(r, chunk)
@@ -498,10 +506,6 @@
             inner = inner - xhat * jnp.mean(d_xhat * xhat, axis=1, keepdims=True)
             o_points[here, :] = (inner * rstd_s[here, 0:1]).astype(BF16)
 
-    with jax.named_scope("sumb_column"):
-        wait(10, rb1.at[pl.ds(0, NXY - 1)])
-        rb2[z] = jnp.sum(rb1[...], axis=0)
-        send_all(11, column, NZ - 1, lambda i: rb2.at[z], rb2.at[z])
     with jax.named_scope("small_column"):
         wait(18, rs1.at[pl.ds(0, NXY - 1)])
         rs2[z] = jnp.sum(rs1[...], axis=0)
@@ -514,11 +518,6 @@
     with jax.named_scope("token_grads"):
         for out, grad in zip((o_q, o_k, o_v), backs):
             out[...] = dot(tokens, grad, 1, 1, HI) / everyone
-    with jax.named_scope("out_last"):
-        wait(17, rp4.at[pl.ds(0, NXY - 1)])
-        o_out[...] = rp4[:, 0].reshape(WIDTH, 128).T
-        for l in range(2):
-            o_feat[:, 128 * l : 128 * l + 128] = rp4[:, 1, 8 * l : 8 * l + 8, :].reshape(128, 128)
     with jax.named_scope("sumb_back"):
         wait(11, rb2.at[pl.ds(0, NZ - 1)])
         rb3[xy] = jnp.sum(rb2[...], axis=0) / everyone
@@ -527,6 +526,11 @@
         wait(19, rs2.at[pl.ds(0, NZ - 1)])
         rs3[xy] = jnp.sum(rs2[...], axis=0) / everyone
         send_all(20, plane, NXY - 1, lambda i: rs3.at[xy], rs3.at[xy])
+    with jax.named_scope("out_last"):
+        wait(17, rp4.at[pl.ds(0, NXY - 1)])
+        o_out[...] = rp4[:, 0].reshape(WIDTH, 128).T
+        for l in range(2):
+            o_feat[:, 128 * l : 128 * l + 128] = rp4[:, 1, 8 * l : 8 * l + 8, :].reshape(128, 128)
     with jax.named_scope("small_last"):
         wait(20, rs3.at[pl.ds(0, NXY - 1)])
         small = [rs3[k // ROWS3, k % ROWS3 : k % ROWS3 + 1, :] for k in range(SMALL)]

time: 62.4 us -> 62 us (level)
  no operation moved by 1% of the time
where the time goes in v6:
time: 62 us; the launch traced here: 61.6 us
  Pallas kernels  60.9 us (98%)
  between operations  0.66 us (1%)
    pallas_call x1, Pallas kernels, shards(): pl.pallas_call(functools.partial(kernel, float(everyone), 256), out_shape...  59.9 us

profile of v6, /device:TPU:1, one launch (start us, length us, event | category | flops | bytes accessed | tf_op | source)
XLA Modules:
  0.0 61.6 jit_solution(11826269672393371699)
XLA Ops:
  0.6 59.9 %backward.1 = (bf16[512,256]{1,0:T(8,128)(2,1)S(1)}, f32[1,256]{1,0:T(1,128)S(1)}, f32[1,256]{1,0:T(1,128)S(1)}, f32[128,256]{1,0:T(8,128)S(1)}, f32[128,256]{1,...) custom-call(bf16[512,256]{1,0:T(8,128)(2,1)} %points_h.1, ...), custom_call_target="tpu_custom_call" | custom-call | tf_op jit(solution)/shard_map/backward/pallas_call | solution.py:603
  60.6 1.0 %hand_on.1 = (bf16[512,256]{1,0:T(8,128)(2,1)}, f32[1,256]{1,0:T(1,128)}, f32[1,256]{1,0:T(1,128)}, f32[128,256]{1,0:T(8,128)}, f32[128,256]{1,0:T(8,128)}, /*in...) custom-call(bf16[512,256]{1,0:T(8,128)(2,1)S(1)} %get-tuple-element., ...), custom_call_target="tpu_custom_call" | custom-call | tf_op jit(solution)/shard_map/hand_on/pallas_call | solution.py:654

commit v7 on v6

--- a/solution.py
+++ b/solution.py
@@ -280,11 +280,8 @@
             ).start()
             return 0
 
-        if count < NXY:
-            for i in range(count):
-                body(i, 0)
-        else:
-            lax.fori_loop(0, count, body, 0)
+        for i in range(count):
+            body(i, 0)
 
     def swap(stage, src, dst):
         send_all(stage, lambda i: sibling, 1, lambda i: src, dst)
@@ -460,11 +457,6 @@
         swap(9, pb.at[1 - c], rb0)
         for r in range(0, rows // 2, chunk):
             norm(r)
-    with jax.named_scope("sumb_plane"):
-        wait(9, rb0)
-        ab[...] = pb[c] + rb0[...]
-        send_all(10, plane, NXY - 1, lambda i: ab.at[plane_index(i)], rb1.at[xy])
-        rb1[xy] = ab[xy]
     with jax.named_scope("shares_small"):
         for r in range(rows // 2, rows, chunk):
             norm(r)
@@ -478,6 +470,12 @@
         for k in range(NXY):
             ps[k] = small[ROWS3 * k : ROWS3 * k + ROWS3]
         swap(0, ps, rs0)
+
+    with jax.named_scope("sumb_plane"):
+        wait(9, rb0)
+        ab[...] = pb[c] + rb0[...]
+        send_all(10, plane, NXY - 1, lambda i: ab.at[plane_index(i)], rb1.at[xy])
+        rb1[xy] = ab[xy]
 
     with jax.named_scope("out_feat"):
         wait(15, rp2.at[pl.ds(0, NZ - 1)])

time: 62 us -> 61.9 us (level)
  no operation moved by 1% of the time
where the time goes in v7:
time: 61.9 us; the launch traced here: 61.2 us
  Pallas kernels  60.5 us (98%)
  between operations  0.66 us (1%)
    pallas_call x1, Pallas kernels, shards(): pl.pallas_call(functools.partial(kernel, float(everyone), 256), out_shape...  59.6 us

profile of v7, /device:TPU:1, one launch (start us, length us, event | category | flops | bytes accessed | tf_op | source)
XLA Modules:
  0.0 61.2 jit_solution(13021370263335350708)
XLA Ops:
  0.6 59.6 %backward.1 = (bf16[512,256]{1,0:T(8,128)(2,1)S(1)}, f32[1,256]{1,0:T(1,128)S(1)}, f32[1,256]{1,0:T(1,128)S(1)}, f32[128,256]{1,0:T(8,128)S(1)}, f32[128,256]{1,...) custom-call(bf16[512,256]{1,0:T(8,128)(2,1)} %points_h.1, ...), custom_call_target="tpu_custom_call" | custom-call | tf_op jit(solution)/shard_map/backward/pallas_call | solution.py:601
  60.2 1.0 %hand_on.1 = (bf16[512,256]{1,0:T(8,128)(2,1)}, f32[1,256]{1,0:T(1,128)}, f32[1,256]{1,0:T(1,128)}, f32[128,256]{1,0:T(8,128)}, f32[128,256]{1,0:T(8,128)}, /*in...) custom-call(bf16[512,256]{1,0:T(8,128)(2,1)S(1)} %get-tuple-element., ...), custom_call_target="tpu_custom_call" | custom-call | tf_op jit(solution)/shard_map/hand_on/pallas_call | solution.py:652
